TPU v7x, 128 devices: a whole 4x4x4 slice. The times are simulated.
128 devices in a mesh: seqhi: 4 (over y), seqlo: 32 (over z, x, core).
Axes of the slice: x: 4, y: 4, z: 4, core: 2. Of those that a mesh axis runs over, the one named last changes fastest.
Arguments:
- query: bfloat16 [32768, 1280], P(('seqhi', 'seqlo')), may hold values from -6 to 6
- key: bfloat16 [32768, 1280], P(('seqhi', 'seqlo')), may hold values from -6 to 6
- value: bfloat16 [32768, 1280], P(('seqhi', 'seqlo')), may hold values from -6 to 6
- grad_out: bfloat16 [32768, 1280], P(('seqhi', 'seqlo')), may hold values from -6 to 6
- offsets: int32 [3, 10], replicated, may hold values from 0 to 63, as said below
Outputs:
- attended: bfloat16 [32768, 1280], P(('seqhi', 'seqlo'))
- grad_query: bfloat16 [32768, 1280], P(('seqhi', 'seqlo'))
- grad_key: bfloat16 [32768, 1280], P(('seqhi', 'seqlo'))
- grad_value: bfloat16 [32768, 1280], P(('seqhi', 'seqlo'))
Inputs may be any that keep to these rules, and one draw needn't show every extreme that they name: offsets[l, h] is below 2^(3 * l); at every level some head has offset 2^(3 * l) - 1.
All inputs are finite; a program needn't handle non-finite values.
Results may differ from a plain program's by a relative error of at most 0.0096.
Values may be sent and summed in bfloat16 or wider, within the bound.
No kernel may reach another device: no remote copies, remote signals or barrier semaphores. Data moves between devices by JAX's collectives and lax.ppermute only.
A program may use at most 192 MiB of HBM per device.

v0:
```python
import functools

import jax
import jax.numpy as jnp
from jax import lax
from jax.experimental import pallas as pl
from jax.experimental.pallas import tpu as pltpu
from jax.sharding import PartitionSpec as P

H = 10
HD = 128
ROWS = 256
SCALING = HD ** -0.5
LOG2E = 1.4426950408889634
FACTOR = SCALING * LOG2E
NEG = -1e30
WIDE = (ROWS, H * HD)
HALF = jnp.bfloat16
FULL = jnp.float32


def swapped(x, axis, mask):
    return lax.ppermute(x, axis, [(i, i ^ mask) for i in range(lax.axis_size(axis))])


def together(*arrays):
    return lax.optimization_barrier(arrays)


def dot_nt(a, b):
    return lax.dot_general(a, b, (((1,), (1,)), ((), ())), preferred_element_type=FULL)


def dot_nn(a, b):
    return lax.dot_general(a, b, (((1,), (0,)), ((), ())), preferred_element_type=FULL)


def grid_ij(shape):
    return (
        lax.broadcasted_iota(jnp.int32, shape, 0),
        lax.broadcasted_iota(jnp.int32, shape, 1),
    )


def eye_column(row, n):
    i, j = grid_ij((n, n))
    return jnp.sum(jnp.where(i == j, row, 0.0), 1, keepdims=True)


def heads_of(step, parts=2):
    return [(step * parts + part, slice(part * HD, (part + 1) * HD)) for part in range(parts)]


def pick_kernel(off_ref, k_ref, v_ref, q_ref, g_ref, out_ref):
    i, p = grid_ij((48, ROWS))
    out_ref[3, :, HD:] = jnp.zeros((144, 2 * HD), HALF)
    for h, lanes in heads_of(0, H):
        z, cols = h // 3, slice(h % 3 * HD, (h % 3 + 1) * HD)
        one = (i < 32) & (p == 8 * i + off_ref[1, h])
        two = (i >= 32) & (p == 64 * (i & 3) + off_ref[2, h])
        rows = [
            dot_nn((one | (two & ((i - 32) // 4 == t))).astype(HALF), r[:, lanes])
            for t, r in enumerate((k_ref, v_ref, q_ref, g_ref))
        ]
        out_ref[z, 0:32, cols] = rows[0][:32].astype(HALF)
        out_ref[z, 32:64, cols] = rows[1][:32].astype(HALF)
        out_ref[z, 64:80, cols] = sum(x[32:] for x in rows).astype(HALF)
        out_ref[z, 80:112, cols] = rows[2][:32].astype(HALF)
        out_ref[z, 112:144, cols] = rows[3][:32].astype(HALF)


def softmax_all(problems):
    scores = [[dot_nt(q, k) * FACTOR for k in keys] for q, keys, _ in problems]
    peaks = [
        functools.reduce(jnp.maximum, [jnp.max(s, 1, keepdims=True) for s in part])
        for part in scores
    ]
    exps = [[jnp.exp2(s - peak) for s in part] for part, peak in zip(scores, peaks)]
    totals = [sum(jnp.sum(e, 1, keepdims=True) for e in part) for part in exps]
    outs = [
        sum(dot_nn(e.astype(HALF), v) for e, v in zip(part, values))
        for part, (_, _, values) in zip(exps, problems)
    ]
    return peaks, totals, outs


def lanes_of(columns):
    _, j = grid_ij((columns[0].shape[0], 128))
    block = jnp.zeros((columns[0].shape[0], 128), FULL)
    for lane, column in enumerate(columns):
        block = jnp.where(j == lane, column, block)
    return block


def near_kernel(q_ref, *refs):
    k_refs, v_refs, (out_ref, stat_ref) = refs[:4], refs[4:8], refs[8:]
    parts = heads_of(0, 5)
    peaks, totals, outs = softmax_all(
        [(q_ref[:, c], [k[:, c] for k in k_refs], [v[:, c] for v in v_refs]) for _, c in parts]
    )
    for (_, c), out, total in zip(parts, outs, totals):
        out_ref[:, c] = out * (1.0 / total)
    block = lanes_of([peak + jnp.log2(total) for peak, total in zip(peaks, totals)])
    stat_ref[0] = block.T[0:8]


def joined(refs, rows, c):
    return jnp.concatenate([r[:, :, rows, c].reshape(256, HD) for r in refs], 0)


def group_rows(a_ref, b_ref, y_ref, c):
    one = {
        "k": a_ref[0, :, 0:32, c], "v": a_ref[0, :, 32:64, c],
        "q": b_ref[0, :, 0:32, c], "g": b_ref[0, :, 32:64, c],
    }
    one = {name: x.reshape(128, HD) for name, x in one.items()}
    two = {name: y_ref[0, t, 0:16, c] for t, name in enumerate("kvqg")}
    return one, two


def group_forward_kernel(zs_ref, *refs):
    a0, a1, (y0, y1, ret_ref) = refs[0:2], refs[2:4], refs[4:]
    problems = []
    parts = heads_of(0, 3)
    for _, c in parts:
        q1 = zs_ref[:, 80:112, c].reshape(128, HD)
        problems.append((
            q1,
            [joined(r, slice(0, 32), c) for r in (a0, a1)],
            [joined(r, slice(32, 64), c) for r in (a0, a1)],
        ))
        problems.append((
            y0[0, 2, 0:16, c],
            [y[:, 0, :, c].reshape(256, HD) for y in (y0, y1)],
            [y[:, 1, :, c].reshape(256, HD) for y in (y0, y1)],
        ))
    peaks, totals, outs = softmax_all(problems)
    outs = [out * (1.0 / total) for out, total in zip(outs, totals)]
    lses = [peak + jnp.log2(total) for peak, total in zip(peaks, totals)]
    one, two = lanes_of(lses[0::2]), lanes_of(lses[1::2])
    for m in range(4):
        for (_, c), out1, out2 in zip(parts, outs[0::2], outs[1::2]):
            ret_ref[m, 0:32, c] = out1[32 * m : 32 * m + 32]
            ret_ref[m, 32:36, c] = out2[4 * m : 4 * m + 4]
        ret_ref[m, 0:32, 384:512] = one[32 * m : 32 * m + 32]
        ret_ref[m, 32:36, 384:512] = two[4 * m : 4 * m + 4]
        ret_ref[m, 36:40, :] = jnp.zeros((4, 512), FULL)


def thirds_of(x):
    pieces = []
    for _ in range(3):
        pieces.append(x.astype(HALF))
        x = x - pieces[-1].astype(FULL)
    return pieces


def row_times(row, onehot):
    i, _ = grid_ij((8, row.shape[1]))
    rows = jnp.zeros((8, row.shape[1]), FULL)
    for n, piece in enumerate(thirds_of(row)):
        rows = jnp.where(i == n, piece.astype(FULL), rows)
    return jnp.sum(dot_nn(rows.astype(HALF), onehot), 0, keepdims=True)


def transposed(rows):
    rows = list(rows)
    width = rows[0].shape[1]
    return jnp.concatenate(rows + [jnp.zeros((128 - len(rows), width), FULL)], 0).T


def merge_kernel(
    off_ref, near_ref, near_stat_ref, g_ref, ret_ref, att_ref, stat_ref, row_ref, sel_ref
):
    lses, scales, picked, far_scales, hits = [], [], [], [], []
    for h in range(H):
        mine = h // 3
        i, p = grid_ij((40, ROWS))
        one = (i < 32) & (p == 8 * i + off_ref[1, h])
        two = (i >= 32) & (i < 36) & (p == 64 * (i - 32) + off_ref[2, h])
        far = ret_ref[mine, :, 384:512].T[h % 3 : h % 3 + 1]
        both = row_times(far, jnp.concatenate([one, two], 1).astype(HALF))
        _, p = grid_ij((1, ROWS))
        lse0 = near_stat_ref[h // 5, h % 5 : h % 5 + 1, :]
        lse1 = jnp.where((p & 7) == off_ref[1, h], both[:, :ROWS], NEG)
        lse2 = jnp.where((p & 63) == off_ref[2, h], both[:, ROWS:], NEG)
        peak = jnp.maximum(jnp.maximum(lse0, lse1), lse2)
        total = jnp.exp2(lse0 - peak) + jnp.exp2(lse1 - peak) + jnp.exp2(lse2 - peak)
        lses.append(peak + jnp.log2(total))
        scales.append(jnp.exp2(lse0 - lses[-1]))
        p, j = grid_ij((ROWS, 128))
        target = jnp.where(j < 32, 8 * j + off_ref[1, h], 64 * (j - 32) + off_ref[2, h])
        hits.append(((p == target) & (j < 36)).astype(HALF))
        picked.append(row_times(lses[-1], hits[-1]))
        _, j = grid_ij((1, 40))
        far_scale = jnp.where(j < 36, jnp.exp2(jnp.minimum(far - picked[-1][:, :40], 1.0)), 0.0)
        far_scales.append(jnp.concatenate([far_scale, jnp.zeros((1, 88), FULL)], 1))
    scales = transposed(scales)
    far_scales = transposed(far_scales)
    dots = []
    for h, c in heads_of(0, H):
        mine, lane = h // 3, slice(h % 3 * HD, (h % 3 + 1) * HD)
        far = ret_ref[mine, :, lane] * far_scales[:40, h : h + 1]
        high = far.astype(HALF)
        low = (far - high.astype(FULL)).astype(HALF)
        lifted = dot_nn(hits[h][:, :40], jnp.concatenate([high, low], 1))
        out = near_ref[:, c] * scales[:, h : h + 1] + lifted[:, :HD] + lifted[:, HD:]
        att_ref[:, c] = out.astype(HALF)
        dots.append(jnp.sum(out * g_ref[:, c].astype(FULL), 1, keepdims=True))
    dots = lanes_of(dots).T
    dots = [dots[h : h + 1] for h in range(H)]
    for s in range(2):
        stat_ref[s] = transposed(lses[5 * s : 5 * s + 5] + dots[5 * s : 5 * s + 5])
    for s in range(5):
        rows = lses[2 * s : 2 * s + 2] + dots[2 * s : 2 * s + 2]
        row_ref[s] = jnp.concatenate(rows + [jnp.zeros((4, ROWS), FULL)], 0)
    picked += [jnp.zeros((1, 128), FULL)] * 2
    dots = [row_times(dots[h], hits[h]) for h in range(H)] + [jnp.zeros((1, 128), FULL)] * 2
    packed = jnp.zeros((8, 128), FULL)
    for j in range(3):
        rows = jnp.concatenate(picked[j::3] + dots[j::3], 0)
        packed = packed + (pltpu.roll(rows, 40 * j, 1) if j else rows)
    for z in range(4):
        block = jnp.concatenate([packed[z : z + 1], packed[4 + z : 5 + z]], 0)
        for i in range(32):
            sel_ref[i // 8 * 32 + 8 * z + i % 8] = block


def gradients(problems):
    probs = [jnp.exp2(dot_nt(a, b) * FACTOR - lse) for a, b, _, _, lse, _ in problems]
    dprobs = [dot_nt(c, d) for _, _, c, d, _, _ in problems]
    return [
        (prob.astype(HALF), (prob * (dprob - row_dot)).astype(HALF))
        for prob, dprob, (_, _, _, _, _, row_dot) in zip(probs, dprobs, problems)
    ]


def near_query_kernel(q_ref, g_ref, stat_ref, *refs):
    k_refs, v_refs, (dq_ref,) = refs[:4], refs[4:8], refs[8:]
    problems = []
    for part, (_, c) in enumerate(heads_of(0, 5)):
        lse = stat_ref[0, :, part : part + 1]
        row_dot = stat_ref[0, :, part + 5 : part + 6]
        for k, v in zip(k_refs, v_refs):
            problems.append((q_ref[:, c], k[:, c], g_ref[:, c], v[:, c], lse, row_dot))
    done = gradients(problems)
    for part, (_, c) in enumerate(heads_of(0, 5)):
        dq_ref[:, c] = sum(dot_nn(ds, k[:, c]) for (_, ds), k in zip(done[4 * part :], k_refs))


def gathered_stats(s_ref, c):
    _, lane = grid_ij((2, 128))
    one = [[], [], []]
    two = [[jnp.zeros((2, 128), FULL)] * 2 for _ in range(3)]

    def moved(rows, distance):
        return pltpu.roll(rows, distance % 128, 1) if distance % 128 else rows

    for y in range(4):
        for x, x_mask in enumerate(MASKS4):
            blocks = [jnp.zeros((2, 128), FULL)] * 3
            for z in range(4):
                source = (lax.axis_index("seqhi") ^ y) * 32 + (
                    8 * z + ((lax.axis_index("seqlo") & 7) ^ (2 * x_mask + c))
                )
                rows = s_ref[source]
                start = 64 * (y % 2) + 16 * x + 4 * z
                for j in range(3):
                    if y == 0:
                        blocks[j] = jnp.where(lane // 32 == z, moved(rows, 32 * z - 40 * j), blocks[j])
                    two[j][y // 2] = jnp.where(
                        (lane >= start) & (lane < start + 4),
                        moved(rows, start - 32 - 40 * j),
                        two[j][y // 2],
                    )
            if y == 0:
                for j in range(3):
                    one[j].append(blocks[j])
    return [jnp.concatenate(x, 1) for x in one], [jnp.concatenate(x, 1) for x in two]


def group_backward_kernel(*refs):
    a0, a1, b0, b1 = refs[0:2], refs[2:4], refs[4:6], refs[6:8]
    y0, y1, s_ref, out_ref = refs[8:]
    problems, others = [], []
    parts = heads_of(0, 3)
    s10, s20 = gathered_stats(s_ref, 0)
    s11, s21 = gathered_stats(s_ref, 1)
    for j, c in parts:
        one, two = group_rows(a0[0], b0[0], y0, c)
        sides = []
        for a, b, s in ((a0, b0, s10), (a1, b1, s11)):
            sides.append((
                joined(a, slice(0, 32), c), joined(a, slice(32, 64), c),
                joined(b, slice(0, 32), c), joined(b, slice(32, 64), c),
                s[j][0:1], s[j][1:2],
            ))
        for y, s in ((y0, s20), (y1, s21)):
            sides.append(
                tuple(y[:, t, :, c].reshape(256, HD) for t in range(4))
                + (s[j][0:1], s[j][1:2]))
        own = (one, one, two, two)
        for rows, n, (k, v, q, g, lse, row_dot) in zip(own, (128, 128, 16, 16), sides):
            first = sides[0] if n == 128 else sides[2]
            lse_own = eye_column(first[4][:, :n], n)
            dot_own = eye_column(first[5][:, :n], n)
            problems.append((rows["q"], k, rows["g"], v, lse_own, dot_own))
            others.append(k)
            problems.append((rows["k"], q, rows["v"], g, lse, row_dot))
            others.append((q, g))
    done = gradients(problems)
    for j, c in parts:
        mine, rest = done[8 * j : 8 * j + 8], others[8 * j : 8 * j + 8]
        dq = [dot_nn(mine[n][1], rest[n]) * SCALING for n in (0, 2, 4, 6)]
        dk = [dot_nn(mine[n][1], rest[n][0]) * SCALING for n in (1, 3, 5, 7)]
        dv = [dot_nn(mine[n][0], rest[n][1]) for n in (1, 3, 5, 7)]
        one = [(x[0] + x[1]).astype(HALF) for x in (dq, dk, dv)]
        two = [x[2] + x[3] for x in (dq, dk, dv)]
        for m in range(4):
            for t in range(3):
                out_ref[m, 32 * t : 32 * t + 32, c] = one[t][32 * m : 32 * m + 32]
            small = [x[4 * m : 4 * m + 4] for x in two] + [jnp.zeros((4, HD), FULL)]
            out_ref[m, 96:112, c] = jnp.concatenate(small, 0).astype(HALF)


def near_key_kernel(k_ref, v_ref, *refs):
    qg_refs, s_refs, (dk_ref, dv_ref) = refs[:4], refs[4:8], refs[8:]
    problems = []
    for part, (_, c) in enumerate(heads_of(0)):
        for qg, s in zip(qg_refs, s_refs):
            lse, row_dot = s[0, part : part + 1, :], s[0, part + 2 : part + 3, :]
            problems.append((k_ref[:, c], qg[0, :, c], v_ref[:, c], qg[1, :, c], lse, row_dot))
    done = gradients(problems)
    for part, (_, c) in enumerate(heads_of(0)):
        mine = done[4 * part : 4 * part + 4]
        dk_ref[:, c] = sum(dot_nn(ds, qg[0, :, c]) for (_, ds), qg in zip(mine, qg_refs))
        dv_ref[:, c] = sum(dot_nn(prob, qg[1, :, c]) for (prob, _), qg in zip(mine, qg_refs))


def add_kernel(
    off_ref, dq_near_ref, dk_near_ref, dv_near_ref, back_ref, dq_ref, dk_ref, dv_ref
):
    p, r = grid_ij((ROWS, 112))
    tensor = jnp.where(r < 96, r // 32, (r - 96) // 4)
    for h, c in heads_of(pl.program_id(0), 5):
        target = jnp.where(r < 96, 8 * (r & 31) + off_ref[1, h], 64 * (r & 3) + off_ref[2, h])
        hit = p == target
        rows = back_ref[h // 3, :, pl.ds(pl.multiple_of(h % 3 * HD, HD), HD)]
        lifted = [dot_nn((hit & (tensor == t)).astype(HALF), rows) for t in range(3)]
        dq_ref[:, c] = (dq_near_ref[:, c] * SCALING + lifted[0]).astype(HALF)
        dk_ref[:, c] = (dk_near_ref[:, c] * SCALING + lifted[1]).astype(HALF)
        dv_ref[:, c] = (dv_near_ref[:, c] + lifted[2]).astype(HALF)


COLUMNS = pl.BlockSpec((ROWS, 2 * HD), lambda s, *_: (0, s))
PAIR = pl.BlockSpec((2, ROWS, 2 * HD), lambda s, *_: (0, 0, s))
FIVE = pl.BlockSpec((ROWS, 5 * HD), lambda s, *_: (0, s))
LANES = pl.BlockSpec((1, ROWS, 128), lambda s, *_: (s, 0, 0))
STAT_ROWS = pl.BlockSpec((1, 8, ROWS), lambda s, *_: (s, 0, 0))


def whole(*shape):
    return pl.BlockSpec(shape, lambda *_: (0,) * len(shape))


def array(*shape, dtype=HALF):
    return jax.ShapeDtypeStruct(shape, dtype)


def call(kernel, name, steps, in_specs, out_specs, out_shape, operands, prefetch=0, room=60, time=0.001):
    return pl.pallas_call(
        kernel,
        grid_spec=pltpu.PrefetchScalarGridSpec(
            num_scalar_prefetch=prefetch, grid=(steps,), in_specs=in_specs, out_specs=out_specs
        ),
        out_shape=out_shape,
        compiler_params=pltpu.CompilerParams(vmem_limit_bytes=room * 1024 * 1024),
        cost_estimate=pl.CostEstimate(flops=int(time * 1_150_000_000), bytes_accessed=100_000, transcendentals=0),
        name=name,
    )(*operands)


CORE, X1, X3 = 1, 2, 6
MASKS4 = (0, 1, 3, 2)
ZS = (8, 16, 24)


def two_steps(x, axis, first, second):
    x = jnp.stack([x, swapped(x, axis, first)])
    return jnp.concatenate([x, swapped(x, axis, second)], 0)


def around(x, axis, masks):
    return [x] + [swapped(x, axis, m) for m in masks]


def over_z(parts):
    groups = [[8 * z + i for z in range(4)] for i in range(8)]
    return lax.all_to_all(parts, "seqlo", 0, 0, axis_index_groups=groups, tiled=True)


def core(x):
    return swapped(x, "seqlo", CORE)


def body(query, key, value, grad_out, offsets):
    kx = swapped(key, "seqlo", X1)
    zs = call(
        pick_kernel, "pick_rows", 1, [whole(*WIDE)] * 4, [whole(4, 144, 384)],
        [array(4, 144, 384)], (offsets, key, value, query, grad_out), prefetch=1,
    )[0]
    zs = over_z(zs)
    a, y, b, kx = together(zs[:, :64], zs[:, 64:80], zs[:, 80:], kx)
    y = jnp.stack([y, swapped(y, "seqlo", X1)])
    a, y, b = together(a, y, b)
    a, b = [jnp.stack([t, swapped(t, "seqlo", X1)]) for t in (a, b)]
    y = jnp.concatenate([y, swapped(y, "seqlo", X3)], 0)
    value_out, a, b, y = together(value, a, b, y)
    vx = swapped(value_out, "seqlo", X1)
    a3 = swapped(a, "seqlo", X3)
    y = y.reshape(4, 4, 4, 4, 384).transpose(2, 0, 1, 3, 4).reshape(4, 64, 384)
    y = around(y, "seqhi", (1, 2, 3))
    a3, *y = together(a3, *y)
    b3 = swapped(b, "seqlo", X3)
    both, vx = together(jnp.stack([query, grad_out]), vx)
    both_x = swapped(both, "seqlo", X1)
    y = jnp.stack(y)
    a, y = [a, a3, core(a), core(a3)], [y, core(y)]
    part_spec, y_spec = whole(2, 4, 64, 384), whole(4, 4, 64, 384)
    (ret,) = call(
        group_forward_kernel, "group_forward", 1,
        [whole(4, 144, 384)] + [part_spec] * 4 + [y_spec] * 2, [whole(4, 40, 512)],
        [array(4, 40, 512, dtype=FULL)], (zs, *a, *y),
    )
    near_query, ret = together(query, ret)
    ret = over_z(ret)
    keys0 = [key, core(key), kx, core(kx)]
    values0 = [value, core(value), vx, core(vx)]
    near, near_stat = call(
        near_kernel, "near_forward", 2, [FIVE] * 9, [FIVE, STAT_ROWS],
        [array(*WIDE, dtype=FULL), array(2, 8, ROWS, dtype=FULL)],
        (near_query, *keys0, *values0),
    )
    ret, near_stat, b3 = together(ret, near_stat, b3)
    attended, stat, rows, sel = call(
        merge_kernel, "merge_levels", 1,
        [whole(*WIDE), whole(2, 8, ROWS), whole(*WIDE), whole(4, 40, 512)],
        [whole(*WIDE), whole(2, ROWS, 128), whole(5, 8, ROWS), whole(128, 2, 128)],
        [
            array(*WIDE), array(2, ROWS, 128, dtype=FULL), array(5, 8, ROWS, dtype=FULL),
            array(128, 2, 128, dtype=FULL),
        ],
        (offsets, near, near_stat, grad_out, ret), prefetch=1,
    )

    sel = lax.all_to_all(sel, ("seqhi", "seqlo"), 0, 0, tiled=True)
    b = [b, b3, core(b), core(b3)]
    sx = swapped(rows, "seqlo", X1)
    stat, both_x = together(stat, both_x)
    both = [both, core(both), both_x, core(both_x)]
    (dq_near,) = call(
        near_query_kernel, "near_query_gradient", 2, [FIVE] * 2 + [LANES] + [FIVE] * 8,
        [FIVE], [array(*WIDE, dtype=FULL)],
        (query, grad_out, stat, *keys0, *values0), time=8,
    )
    sel, dq_near = together(sel, dq_near)
    (back,) = call(
        group_backward_kernel, "group_backward", 1,
        [part_spec] * 8 + [y_spec] * 2 + [whole(128, 2, 128)],
        [whole(4, 112, 384)], [array(4, 112, 384)],
        (*a, *b, *y, sel),
    )
    sx, back = together(sx, back)
    s0 = [rows, core(rows), sx, core(sx)]
    dk_near, dv_near = call(
        near_key_kernel, "near_key_gradient", 5, [COLUMNS] * 2 + [PAIR] * 4 + [STAT_ROWS] * 4, [COLUMNS] * 2,
        [array(*WIDE, dtype=FULL)] * 2, (key, value, *both, *s0),
    )
    back = over_z(back)
    back, dk_near = together(back, dk_near)
    grad_query, grad_key, grad_value = call(
        add_kernel, "add_levels", 2,
        [FIVE] * 3 + [whole(4, 112, 384)], [FIVE] * 3, [array(*WIDE)] * 3,
        (offsets, dq_near, dk_near, dv_near, back), prefetch=1,
    )
    return attended, grad_query, grad_key, grad_value


def solution(mesh):
    spec = P(("seqhi", "seqlo"), None)
    return jax.shard_map(
        body,
        mesh=mesh,
        in_specs=(spec, spec, spec, spec, P()),
        out_specs=(spec, spec, spec, spec),
        check_vma=False,
    )
```

profile of v0, /device:TPU:1, one launch (start us, length us, event | category | flops | bytes accessed | tf_op | source)
XLA Modules:
  0.0 125.6 jit_solution(14928689941734807403)
XLA Ops:
  0.6 2.1 %collective-permute-start = (bf16[256,1280]{1,0:T(8,128)(2,1)}, bf16[256,1280]{1,0:T(8,128)(2,1)}, u32[]{:S(2)}, u32[]{:S(2)}) collective-permute-start(bf16[256,1280]{1,0:T(8,128)(2,1)} %k_ref.3), channel_id=1, source_target_pairs={{0,2},{1,3},{2,0},{3,1},{4,6},{5,7},{6,4},{7,5},{8,10},{9,11},{10,... | collective-permute-start | bytes 1966088 | tf_op jit(solution)/shard_map/ppermute | solution.py:23
  2.8 3.6 %pick_rows.1 = bf16[4,144,384]{2,1,0:T(8,128)(2,1)} custom-call(s32[3,10]{1,0:T(4,128)} %off_ref.5, bf16[256,1280]{1,0:T(8,128)(2,1)} %k_ref.3, bf16[256,1280]{1,0:T(8,128)(2,1)} %v_ref.3, bf16[256,1280]{1,0:T(8,128)(2,1)} %q_ref.4, bf16[256,1280]{1,0:T(8,128)(2,1)} %g_ref.5), custom_call_target="tpu_custom_call" | custom-call | flops 1150000 | bytes 100000 | tf_op jit(solution)/shard_map/pick_rows/pallas_call | solution.py:371
  6.4 12.4 %all_to_all.20.zs_ref = bf16[4,144,384]{2,1,0:T(8,128)(2,1)S(1)} all-to-all(bf16[4,144,384]{2,1,0:T(8,128)(2,1)} %pick_rows.1), channel_id=1, replica_groups={{0,8,16,24},{1,9,17,25},{2,10,18,26},{3,11,19,27},{4,12,20,28},{5,13,21..., dimensions={0} | all-to-all | bytes 884736 | tf_op jit(solution)/shard_map/all_to_all | solution.py:399
  19.2 2.7 %collective-permute-done.1 = bf16[4,16,384]{2,1,0:T(8,128)(2,1)S(1)} collective-permute-done((bf16[4,16,384]{2,1,0:T(8,128)(2,1)S(1)}, bf16[4,16,384]{2,1,0:T(8,128)(2,1)S(1)}, u32[]{:S(2)}, u32[]{:S(2)}) %collective-permute-start.1) | collective-permute-done | bytes 49184 | tf_op jit(solution)/shard_map/ppermute | solution.py:23
  21.9 1.9 %collective-permute-start.4 = (bf16[2,4,16,384]{3,2,1,0:T(8,128)(2,1)S(1)}, bf16[2,4,16,384]{3,2,1,0:T(8,128)(2,1)S(1)}, u32[]{:S(2)}, u32[]{:S(2)}) collective-permute-start(bf16[2,4,16,384]{3,2,1,0:T(8,128)(2,1)S(1)} %pad_maximum_fusion.5), channel_id=1, source_target_pairs={{0,6},{1,7},{2,4},{3,5},{4,2},{5,3},{6,0},{7,1},{8,14},{9,15},{10,... | collective-permute-start | bytes 294920 | tf_op jit(solution)/shard_map/ppermute | solution.py:23
  25.3 1.4 %collective-permute-done.4 = bf16[2,4,16,384]{3,2,1,0:T(8,128)(2,1)S(1)} collective-permute-done((bf16[2,4,16,384]{3,2,1,0:T(8,128)(2,1)S(1)}, bf16[2,4,16,384]{3,2,1,0:T(8,128)(2,1)S(1)}, u32[]{:S(2)}, u32[]{:S(2)}) %collective-permute-start.4) | collective-permute-done | bytes 98336 | tf_op jit(solution)/shard_map/ppermute | solution.py:23
  26.7 1.6 %collective-permute-done.3 = bf16[4,64,384]{2,1,0:T(8,128)(2,1)S(1)} collective-permute-done((bf16[4,64,384]{2,1,0:T(8,128)(2,1)S(1)}, bf16[4,64,384]{2,1,0:T(8,128)(2,1)S(1)}, u32[]{:S(2)}, u32[]{:S(2)}) %collective-permute-start.3) | collective-permute-done | bytes 196640 | tf_op jit(solution)/shard_map/ppermute | solution.py:23
  28.4 2.4 %collective-permute-done.2 = bf16[4,64,384]{2,1,0:T(8,128)(2,1)S(1)} collective-permute-done((bf16[4,64,384]{2,1,0:T(8,128)(2,1)S(1)}, bf16[4,64,384]{2,1,0:T(8,128)(2,1)S(1)}, u32[]{:S(2)}, u32[]{:S(2)}) %collective-permute-start.2) | collective-permute-done | bytes 196640 | tf_op jit(solution)/shard_map/ppermute | solution.py:23
  34.0 1.4 %collective-permute-start.6 = (bf16[4,64,384]{2,1,0:T(8,128)(2,1)S(1)}, bf16[4,64,384]{2,1,0:T(8,128)(2,1)S(1)}, u32[]{:S(2)}, u32[]{:S(2)}) collective-permute-start(bf16[4,64,384]{2,1,0:T(8,128)(2,1)S(1)} %reshape.15), channel_id=1, source_target_pairs={{0,32},{32,0},{64,96},{96,64},{1,33},{33,1},{65,97},{97,65},{2,34}... | collective-permute-start | bytes 589832 | tf_op jit(solution)/shard_map/ppermute | solution.py:23
  35.4 2.6 %collective-permute-start.7 = (bf16[4,64,384]{2,1,0:T(8,128)(2,1)S(1)}, bf16[4,64,384]{2,1,0:T(8,128)(2,1)S(1)}, u32[]{:S(2)}, u32[]{:S(2)}) collective-permute-start(bf16[4,64,384]{2,1,0:T(8,128)(2,1)S(1)} %reshape.15), channel_id=1, source_target_pairs={{0,64},{32,96},{64,0},{96,32},{1,65},{33,97},{65,1},{97,33},{2,66}... | collective-permute-start | bytes 589832 | tf_op jit(solution)/shard_map/ppermute | solution.py:23
  39.3 6.7 %collective-permute-start.12 = (bf16[256,1280]{1,0:T(8,128)(2,1)S(1)}, bf16[256,1280]{1,0:T(8,128)(2,1)S(1)}, u32[]{:S(2)}, u32[]{:S(2)}) collective-permute-start(bf16[256,1280]{1,0:T(8,128)(2,1)S(1)} %copy-done.3), channel_id=1, source_target_pairs={{0,1},{1,0},{2,3},{3,2},{4,5},{5,4},{6,7},{7,6},{8,9},{9,8},{10,11... | collective-permute-start | bytes 1966088 | tf_op jit(solution)/shard_map/ppermute | solution.py:23
  47.1 6.7 %collective-permute-start.11 = (bf16[4,4,64,384]{3,2,1,0:T(8,128)(2,1)S(1)}, bf16[4,4,64,384]{3,2,1,0:T(8,128)(2,1)S(1)}, u32[]{:S(2)}, u32[]{:S(2)}) collective-permute-start(bf16[4,4,64,384]{3,2,1,0:T(8,128)(2,1)S(1)} %pad_maximum_fusion.1.refs_4_.refs_8_), channel_id=1, source_target_pairs={{0,1},{1,0},{2,3},{3,2},{4,5},{5,4},{6,7},{7,6},{8,9},{9,8},{10,11... | collective-permute-start | bytes 2359304 | tf_op jit(solution)/shard_map/ppermute | solution.py:23
  54.4 2.4 %collective-permute-done.9.refs_2_ = bf16[2,4,64,384]{3,2,1,0:T(8,128)(2,1)S(1)} collective-permute-done((bf16[2,4,64,384]{3,2,1,0:T(8,128)(2,1)S(1)}, bf16[2,4,64,384]{3,2,1,0:T(8,128)(2,1)S(1)}, u32[]{:S(2)}, u32[]{:S(2)}) %collective-permute-start.9) | collective-permute-done | bytes 393248 | tf_op jit(solution)/shard_map/ppermute | solution.py:23
  58.1 1.9 %collective-permute-start.17 = (bf16[2,4,64,384]{3,2,1,0:T(8,128)(2,1)S(1)}, bf16[2,4,64,384]{3,2,1,0:T(8,128)(2,1)}, u32[]{:S(2)}, u32[]{:S(2)}) collective-permute-start(bf16[2,4,64,384]{3,2,1,0:T(8,128)(2,1)S(1)} %pad_maximum_fusion.3.refs_4_), channel_id=1, source_target_pairs={{0,6},{1,7},{2,4},{3,5},{4,2},{5,3},{6,0},{7,1},{8,14},{9,15},{10,... | collective-permute-start | bytes 1179656 | tf_op jit(solution)/shard_map/ppermute | solution.py:23
  60.0 3.6 %group_forward.1 = f32[4,40,512]{2,1,0:T(8,128)} custom-call(bf16[4,144,384]{2,1,0:T(8,128)(2,1)} %copy-done.5, bf16[2,4,64,384]{3,2,1,0:T(8,128)(2,1)} %copy-done.6, bf16[2,4,64,384]{3,2,1,0:T(8,128)(2,1)} %copy-done.10, bf16[2,4,64,384]{3,2,1,0:T(8,128)(2,1)} %copy-done.11, bf16[2,4,64,384]{3,2,1,0:T(8,128)(2,1)} %copy-done.12, ...), custom_call_target="tpu_custom_call" | custom-call | flops 1150000 | bytes 100000 | tf_op jit(solution)/shard_map/group_forward/pallas_call | solution.py:371
  63.7 3.6 %all-to-all-start.1 = ((f32[4,40,512]{2,1,0:T(8,128)}), f32[4,40,512]{2,1,0:T(8,128)S(1)}, u32[]{:S(2)}, u32[]{:S(2)}) async-start(f32[4,40,512]{2,1,0:T(8,128)} %group_forward.1), calls=%async_computation.1 | async-start | bytes 655360 | tf_op jit(solution)/shard_map/all_to_all | solution.py:399
  68.0 7.1 %near_forward.1 = (f32[256,1280]{1,0:T(8,128)}, f32[2,8,256]{2,1,0:T(8,128)}) custom-call(bf16[256,1280]{1,0:T(8,128)(2,1)} %q_ref.4, bf16[256,1280]{1,0:T(8,128)(2,1)} %k_ref.3, bf16[256,1280]{1,0:T(8,128)(2,1)} %copy-done.16, bf16[256,1280]{1,0:T(8,128)(2,1)} %collective-permute-done.refs_2_, bf16[256,1280]{1,0:T(8,128)(2,1)} %collective-permute-done.13.refs_3_, ...), custom_call_target="tpu_custom_call" | custom-call | flops 1150000 | bytes 100000 | tf_op jit(solution)/shard_map/near_forward/pallas_call | solution.py:371
  75.8 5.4 %merge_levels.1 = (bf16[256,1280]{1,0:T(8,128)(2,1)}, f32[2,256,128]{2,1,0:T(8,128)}, f32[5,8,256]{2,1,0:T(8,128)}, f32[128,2,128]{2,1,0:T(2,128)}) custom-call(s32[3,10]{1,0:T(4,128)} %off_ref.5, f32[256,1280]{1,0:T(8,128)} %get-tuple-element.63.near_ref, f32[2,8,256]{2,1,0:T(8,128)} %get-tuple-element.67.near_stat_ref, bf16[256,1280]{1,0:T(8,128)(2,1)} %g_ref.5, ...), custom_call_target="tpu_custom_call" | custom-call | flops 1150000 | bytes 100000 | tf_op jit(solution)/shard_map/merge_levels/pallas_call | solution.py:371
  81.8 6.0 %all-to-all-start.2 = ((f32[128,2,128]{2,1,0:T(2,128)}), f32[128,2,128]{2,1,0:T(2,128)S(1)}, u32[]{:S(2)}, u32[]{:S(2)}) async-start(f32[128,2,128]{2,1,0:T(2,128)} %get-tuple-element.70), calls=%async_computation.2 | async-start | bytes 262144 | tf_op jit(solution)/shard_map/all_to_all | solution.py:456
  89.6 7.5 %near_query_gradient.1.dq_near_ref = f32[256,1280]{1,0:T(8,128)} custom-call(bf16[256,1280]{1,0:T(8,128)(2,1)} %q_ref.4, bf16[256,1280]{1,0:T(8,128)(2,1)} %g_ref.5, f32[2,256,128]{2,1,0:T(8,128)} %get-tuple-element.73.stat_ref, bf16[256,1280]{1,0:T(8,128)(2,1)} %k_ref.3, bf16[256,1280]{1,0:T(8,128)(2,1)} %copy-done.16, ...), custom_call_target="tpu_custom_call" | custom-call | flops 9200000000 | bytes 100000 | tf_op jit(solution)/shard_map/near_query_gradient/pallas_call | solution.py:371
  99.3 5.7 %group_backward.1 = bf16[4,112,384]{2,1,0:T(8,128)(2,1)} custom-call(bf16[2,4,64,384]{3,2,1,0:T(8,128)(2,1)} %copy-done.6, bf16[2,4,64,384]{3,2,1,0:T(8,128)(2,1)} %copy-done.10, bf16[2,4,64,384]{3,2,1,0:T(8,128)(2,1)} %copy-done.11, bf16[2,4,64,384]{3,2,1,0:T(8,128)(2,1)} %copy-done.12, bf16[2,4,64,384]{3,2,1,0:T(8,128)(2,1)} %copy-done.9, ...), custom_call_target="tpu_custom_call" | custom-call | flops 1150000 | bytes 100000 | tf_op jit(solution)/shard_map/group_backward/pallas_call | solution.py:371
  104.9 3.8 %all-to-all-start.3 = ((bf16[4,112,384]{2,1,0:T(8,128)(2,1)}), bf16[4,112,384]{2,1,0:T(8,128)(2,1)S(1)}, u32[]{:S(2)}, u32[]{:S(2)}) async-start(bf16[4,112,384]{2,1,0:T(8,128)(2,1)} %group_backward.1), calls=%async_computation.3 | async-start | bytes 688128 | tf_op jit(solution)/shard_map/all_to_all | solution.py:399
  111.5 8.9 %near_key_gradient.1 = (f32[256,1280]{1,0:T(8,128)}, f32[256,1280]{1,0:T(8,128)}) custom-call(bf16[256,1280]{1,0:T(8,128)(2,1)} %k_ref.3, bf16[256,1280]{1,0:T(8,128)(2,1)} %v_ref.3, bf16[2,256,1280]{2,1,0:T(8,128)(2,1)} %pad_maximum_fusion.refs_0_, bf16[2,256,1280]{2,1,0:T(8,128)(2,1)} %copy-done.14, bf16[2,256,1280]{2,1,0:T(8,128)(2,1)} %collective-permute-done.18.refs_2_, ...), custom_call_target="tpu_custom_call" | custom-call | flops 1150000 | bytes 100000 | tf_op jit(solution)/shard_map/near_key_gradient/pallas_call | solution.py:371
  121.1 4.6 %add_levels.1 = (bf16[256,1280]{1,0:T(8,128)(2,1)}, bf16[256,1280]{1,0:T(8,128)(2,1)}, bf16[256,1280]{1,0:T(8,128)(2,1)}) custom-call(s32[3,10]{1,0:T(4,128)} %off_ref.5, f32[256,1280]{1,0:T(8,128)} %near_query_gradient.1.dq_near_ref, f32[256,1280]{1,0:T(8,128)} %get-tuple-element.82.dk_near_ref, f32[256,1280]{1,0:T(8,128)} %get-tuple-element.83.dv_near_ref, ...), custom_call_target="tpu_custom_call" | custom-call | flops 1150000 | bytes 100000 | tf_op jit(solution)/shard_map/add_levels/pallas_call | solution.py:371
  (102 shorter events, 18.9 us)
Async XLA Ops:
  0.6 18.2 %collective-permute-start = (bf16[256,1280]{1,0:T(8,128)(2,1)}, bf16[256,1280]{1,0:T(8,128)(2,1)}, u32[]{:S(2)}, u32[]{:S(2)}) collective-permute-start(bf16[256,1280]{1,0:T(8,128)(2,1)} %k_ref.3), channel_id=1, source_target_pairs={{0,2},{1,3},{2,0},{3,1},{4,6},{5,7},{6,4},{7,5},{8,10},{9,11},{10,... | collective-permute-start | bytes 1966088 | tf_op jit(solution)/shard_map/ppermute | solution.py:23
  21.9 4.8 %collective-permute-start.4 = (bf16[2,4,16,384]{3,2,1,0:T(8,128)(2,1)S(1)}, bf16[2,4,16,384]{3,2,1,0:T(8,128)(2,1)S(1)}, u32[]{:S(2)}, u32[]{:S(2)}) collective-permute-start(bf16[2,4,16,384]{3,2,1,0:T(8,128)(2,1)S(1)} %pad_maximum_fusion.5), channel_id=1, source_target_pairs={{0,6},{1,7},{2,4},{3,5},{4,2},{5,3},{6,0},{7,1},{8,14},{9,15},{10,... | collective-permute-start | bytes 294920 | tf_op jit(solution)/shard_map/ppermute | solution.py:23
  23.8 4.5 %collective-permute-start.3 = (bf16[4,64,384]{2,1,0:T(8,128)(2,1)S(1)}, bf16[4,64,384]{2,1,0:T(8,128)(2,1)S(1)}, u32[]{:S(2)}, u32[]{:S(2)}) collective-permute-start(bf16[4,64,384]{2,1,0:T(8,128)(2,1)S(1)} %get-tuple-element.50), channel_id=1, source_target_pairs={{0,2},{1,3},{2,0},{3,1},{4,6},{5,7},{6,4},{7,5},{8,10},{9,11},{10,... | collective-permute-start | bytes 589832 | tf_op jit(solution)/shard_map/ppermute | solution.py:23
  24.1 6.7 %collective-permute-start.2 = (bf16[4,64,384]{2,1,0:T(8,128)(2,1)S(1)}, bf16[4,64,384]{2,1,0:T(8,128)(2,1)S(1)}, u32[]{:S(2)}, u32[]{:S(2)}) collective-permute-start(bf16[4,64,384]{2,1,0:T(8,128)(2,1)S(1)} %get-tuple-element.49), channel_id=1, source_target_pairs={{0,2},{1,3},{2,0},{3,1},{4,6},{5,7},{6,4},{7,5},{8,10},{9,11},{10,... | collective-permute-start | bytes 589832 | tf_op jit(solution)/shard_map/ppermute | solution.py:23
  30.9 15.1 %collective-permute-start.15 = (bf16[256,1280]{1,0:T(8,128)(2,1)S(1)}, bf16[256,1280]{1,0:T(8,128)(2,1)}, u32[]{:S(2)}, u32[]{:S(2)}) collective-permute-start(bf16[256,1280]{1,0:T(8,128)(2,1)S(1)} %copy-done.4), channel_id=1, source_target_pairs={{0,2},{1,3},{2,0},{3,1},{4,6},{5,7},{6,4},{7,5},{8,10},{9,11},{10,... | collective-permute-start | bytes 1966088 | tf_op jit(solution)/shard_map/ppermute | solution.py:23
  31.2 14.7 %collective-permute-start.5 = (bf16[2,4,64,384]{3,2,1,0:T(8,128)(2,1)S(1)}, bf16[2,4,64,384]{3,2,1,0:T(8,128)(2,1)S(1)}, u32[]{:S(2)}, u32[]{:S(2)}) collective-permute-start(bf16[2,4,64,384]{3,2,1,0:T(8,128)(2,1)S(1)} %pad_maximum_fusion.2.refs_0_), channel_id=1, source_target_pairs={{0,6},{1,7},{2,4},{3,5},{4,2},{5,3},{6,0},{7,1},{8,14},{9,15},{10,... | collective-permute-start | bytes 1179656 | tf_op jit(solution)/shard_map/ppermute | solution.py:23
  34.0 5.2 %collective-permute-start.6 = (bf16[4,64,384]{2,1,0:T(8,128)(2,1)S(1)}, bf16[4,64,384]{2,1,0:T(8,128)(2,1)S(1)}, u32[]{:S(2)}, u32[]{:S(2)}) collective-permute-start(bf16[4,64,384]{2,1,0:T(8,128)(2,1)S(1)} %reshape.15), channel_id=1, source_target_pairs={{0,32},{32,0},{64,96},{96,64},{1,33},{33,1},{65,97},{97,65},{2,34}... | collective-permute-start | bytes 589832 | tf_op jit(solution)/shard_map/ppermute | solution.py:23
  35.4 10.5 %collective-permute-start.7 = (bf16[4,64,384]{2,1,0:T(8,128)(2,1)S(1)}, bf16[4,64,384]{2,1,0:T(8,128)(2,1)S(1)}, u32[]{:S(2)}, u32[]{:S(2)}) collective-permute-start(bf16[4,64,384]{2,1,0:T(8,128)(2,1)S(1)} %reshape.15), channel_id=1, source_target_pairs={{0,64},{32,96},{64,0},{96,32},{1,65},{33,97},{65,1},{97,33},{2,66}... | collective-permute-start | bytes 589832 | tf_op jit(solution)/shard_map/ppermute | solution.py:23
  38.0 7.9 %collective-permute-start.8 = (bf16[4,64,384]{2,1,0:T(8,128)(2,1)S(1)}, bf16[4,64,384]{2,1,0:T(8,128)(2,1)S(1)}, u32[]{:S(2)}, u32[]{:S(2)}) collective-permute-start(bf16[4,64,384]{2,1,0:T(8,128)(2,1)S(1)} %reshape.15), channel_id=1, source_target_pairs={{0,96},{32,64},{64,32},{96,0},{1,97},{33,65},{65,33},{97,1},{2,98}... | collective-permute-start | bytes 589832 | tf_op jit(solution)/shard_map/ppermute | solution.py:23
  39.3 15.0 %collective-permute-start.12 = (bf16[256,1280]{1,0:T(8,128)(2,1)S(1)}, bf16[256,1280]{1,0:T(8,128)(2,1)S(1)}, u32[]{:S(2)}, u32[]{:S(2)}) collective-permute-start(bf16[256,1280]{1,0:T(8,128)(2,1)S(1)} %copy-done.3), channel_id=1, source_target_pairs={{0,1},{1,0},{2,3},{3,2},{4,5},{5,4},{6,7},{7,6},{8,9},{9,8},{10,11... | collective-permute-start | bytes 1966088 | tf_op jit(solution)/shard_map/ppermute | solution.py:23
  46.0 35.2 %collective-permute-start.18 = (bf16[2,256,1280]{2,1,0:T(8,128)(2,1)}, bf16[2,256,1280]{2,1,0:T(8,128)(2,1)}, u32[]{:S(2)}, u32[]{:S(2)}) collective-permute-start(bf16[2,256,1280]{2,1,0:T(8,128)(2,1)} %pad_maximum_fusion.refs_0_), channel_id=1, source_target_pairs={{0,2},{1,3},{2,0},{3,1},{4,6},{5,7},{6,4},{7,5},{8,10},{9,11},{10,... | collective-permute-start | bytes 3932168 | tf_op jit(solution)/shard_map/ppermute | solution.py:23
  47.1 11.0 %collective-permute-start.11 = (bf16[4,4,64,384]{3,2,1,0:T(8,128)(2,1)S(1)}, bf16[4,4,64,384]{3,2,1,0:T(8,128)(2,1)S(1)}, u32[]{:S(2)}, u32[]{:S(2)}) collective-permute-start(bf16[4,4,64,384]{3,2,1,0:T(8,128)(2,1)S(1)} %pad_maximum_fusion.1.refs_4_.refs_8_), channel_id=1, source_target_pairs={{0,1},{1,0},{2,3},{3,2},{4,5},{5,4},{6,7},{7,6},{8,9},{9,8},{10,11... | collective-permute-start | bytes 2359304 | tf_op jit(solution)/shard_map/ppermute | solution.py:23
  54.3 13.0 %collective-permute-start.14 = (bf16[256,1280]{1,0:T(8,128)(2,1)S(1)}, bf16[256,1280]{1,0:T(8,128)(2,1)}, u32[]{:S(2)}, u32[]{:S(2)}) collective-permute-start(bf16[256,1280]{1,0:T(8,128)(2,1)S(1)} %copy-done.4), channel_id=1, source_target_pairs={{0,1},{1,0},{2,3},{3,2},{4,5},{5,4},{6,7},{7,6},{8,9},{9,8},{10,11... | collective-permute-start | bytes 1966088 | tf_op jit(solution)/shard_map/ppermute | solution.py:23
  56.8 11.2 %collective-permute-start.13 = (bf16[256,1280]{1,0:T(8,128)(2,1)}, bf16[256,1280]{1,0:T(8,128)(2,1)}, u32[]{:S(2)}, u32[]{:S(2)}) collective-permute-start(bf16[256,1280]{1,0:T(8,128)(2,1)} %collective-permute-done.refs_2_), channel_id=1, source_target_pairs={{0,1},{1,0},{2,3},{3,2},{4,5},{5,4},{6,7},{7,6},{8,9},{9,8},{10,11... | collective-permute-start | bytes 1966088 | tf_op jit(solution)/shard_map/ppermute | solution.py:23
  57.7 10.2 %collective-permute-start.16 = (bf16[256,1280]{1,0:T(8,128)(2,1)}, bf16[256,1280]{1,0:T(8,128)(2,1)}, u32[]{:S(2)}, u32[]{:S(2)}) collective-permute-start(bf16[256,1280]{1,0:T(8,128)(2,1)} %collective-permute-done.15.refs_6_), channel_id=1, source_target_pairs={{0,1},{1,0},{2,3},{3,2},{4,5},{5,4},{6,7},{7,6},{8,9},{9,8},{10,11... | collective-permute-start | bytes 1966088 | tf_op jit(solution)/shard_map/ppermute | solution.py:23
  58.1 16.9 %collective-permute-start.17 = (bf16[2,4,64,384]{3,2,1,0:T(8,128)(2,1)S(1)}, bf16[2,4,64,384]{3,2,1,0:T(8,128)(2,1)}, u32[]{:S(2)}, u32[]{:S(2)}) collective-permute-start(bf16[2,4,64,384]{3,2,1,0:T(8,128)(2,1)S(1)} %pad_maximum_fusion.3.refs_4_), channel_id=1, source_target_pairs={{0,6},{1,7},{2,4},{3,5},{4,2},{5,3},{6,0},{7,1},{8,14},{9,15},{10,... | collective-permute-start | bytes 1179656 | tf_op jit(solution)/shard_map/ppermute | solution.py:23
  63.7 11.4 %all-to-all-start.1 = ((f32[4,40,512]{2,1,0:T(8,128)}), f32[4,40,512]{2,1,0:T(8,128)S(1)}, u32[]{:S(2)}, u32[]{:S(2)}) async-start(f32[4,40,512]{2,1,0:T(8,128)} %group_forward.1), calls=%async_computation.1 | async-start | bytes 655360 | tf_op jit(solution)/shard_map/all_to_all | solution.py:399
  67.2 43.1 %collective-permute-start.22 = (bf16[2,256,1280]{2,1,0:T(8,128)(2,1)}, bf16[2,256,1280]{2,1,0:T(8,128)(2,1)S(1)}, u32[]{:S(2)}, u32[]{:S(2)}) collective-permute-start(bf16[2,256,1280]{2,1,0:T(8,128)(2,1)} %pad_maximum_fusion.refs_0_), channel_id=1, source_target_pairs={{0,1},{1,0},{2,3},{3,2},{4,5},{5,4},{6,7},{7,6},{8,9},{9,8},{10,11... | collective-permute-start | bytes 3932168 | tf_op jit(solution)/shard_map/ppermute | solution.py:23
  81.2 29.5 %collective-permute-start.23 = (bf16[2,256,1280]{2,1,0:T(8,128)(2,1)}, bf16[2,256,1280]{2,1,0:T(8,128)(2,1)}, u32[]{:S(2)}, u32[]{:S(2)}) collective-permute-start(bf16[2,256,1280]{2,1,0:T(8,128)(2,1)} %collective-permute-done.18.refs_2_), channel_id=1, source_target_pairs={{0,1},{1,0},{2,3},{3,2},{4,5},{5,4},{6,7},{7,6},{8,9},{9,8},{10,11... | collective-permute-start | bytes 3932168 | tf_op jit(solution)/shard_map/ppermute | solution.py:23
  81.7 16.1 %collective-permute-start.20 = (bf16[2,4,64,384]{3,2,1,0:T(8,128)(2,1)S(1)}, bf16[2,4,64,384]{3,2,1,0:T(8,128)(2,1)S(1)}, u32[]{:S(2)}, u32[]{:S(2)}) collective-permute-start(bf16[2,4,64,384]{3,2,1,0:T(8,128)(2,1)S(1)} %pad_maximum_fusion.3.refs_4_), channel_id=1, source_target_pairs={{0,1},{1,0},{2,3},{3,2},{4,5},{5,4},{6,7},{7,6},{8,9},{9,8},{10,11... | collective-permute-start | bytes 1179656 | tf_op jit(solution)/shard_map/ppermute | solution.py:23
  81.8 16.0 %all-to-all-start.2 = ((f32[128,2,128]{2,1,0:T(2,128)}), f32[128,2,128]{2,1,0:T(2,128)S(1)}, u32[]{:S(2)}, u32[]{:S(2)}) async-start(f32[128,2,128]{2,1,0:T(2,128)} %get-tuple-element.70), calls=%async_computation.2 | async-start | bytes 262144 | tf_op jit(solution)/shard_map/all_to_all | solution.py:456
  87.8 10.0 %collective-permute-start.21 = (bf16[2,4,64,384]{3,2,1,0:T(8,128)(2,1)}, bf16[2,4,64,384]{3,2,1,0:T(8,128)(2,1)S(1)}, u32[]{:S(2)}, u32[]{:S(2)}) collective-permute-start(bf16[2,4,64,384]{3,2,1,0:T(8,128)(2,1)} %collective-permute-done.17.refs_5_), channel_id=1, source_target_pairs={{0,1},{1,0},{2,3},{3,2},{4,5},{5,4},{6,7},{7,6},{8,9},{9,8},{10,11... | collective-permute-start | bytes 1179656 | tf_op jit(solution)/shard_map/ppermute | solution.py:23
  88.9 16.0 %collective-permute-start.19 = (f32[5,8,256]{2,1,0:T(8,128)}, f32[5,8,256]{2,1,0:T(8,128)S(1)}, u32[]{:S(2)}, u32[]{:S(2)}) collective-permute-start(f32[5,8,256]{2,1,0:T(8,128)} %get-tuple-element.75.refs_4_), channel_id=1, source_target_pairs={{0,2},{1,3},{2,0},{3,1},{4,6},{5,7},{6,4},{7,5},{8,10},{9,11},{10,... | collective-permute-start | bytes 122888 | tf_op jit(solution)/shard_map/ppermute | solution.py:23
  104.9 15.4 %all-to-all-start.3 = ((bf16[4,112,384]{2,1,0:T(8,128)(2,1)}), bf16[4,112,384]{2,1,0:T(8,128)(2,1)S(1)}, u32[]{:S(2)}, u32[]{:S(2)}) async-start(bf16[4,112,384]{2,1,0:T(8,128)(2,1)} %group_backward.1), calls=%async_computation.3 | async-start | bytes 688128 | tf_op jit(solution)/shard_map/all_to_all | solution.py:399
  (29 other events, 195.3 us)
where the time goes:
time: 126 us
  Pallas kernels  46.4 us (37%)
  starting transfers between devices  46 us (37%)
  waiting for transfers between devices  12.9 us (10%)
  blocking collectives  12.4 us (10%)
  local copies, waits for them, and re-layouts  5.63 us (4%)
  other arithmetic  1.47 us (1%)
    pallas_call x8, Pallas kernels, call(): pl.pallas_call(kernel, grid_spec=pltpu.PrefetchScalarGridSpec(num_scalar_...  46.4 us
    ppermute x26, starting transfers between devices, swapped(): lax.ppermute(x, axis, [(i, i ^ mask) for i in range(lax.axis_size(axis))])  32.6 us
    all_to_all x1, blocking collectives, over_z(): lax.all_to_all(parts, 'seqlo', 0, 0, axis_index_groups=groups, tiled=True)  12.4 us
    ppermute x26, waiting for transfers between devices, swapped(): lax.ppermute(x, axis, [(i, i ^ mask) for i in range(lax.axis_size(axis))])  12.3 us
    all_to_all x2, starting transfers between devices, over_z(): lax.all_to_all(parts, 'seqlo', 0, 0, axis_index_groups=groups, tiled=True)  7.38 us
    all_to_all x1, starting transfers between devices, body(): sel = lax.all_to_all(sel, ('seqhi', 'seqlo'), 0, 0, tiled=True)  5.99 us
    unnamed x48, local copies, waits for them, and re-layouts  3.81 us
  transfers between devices with their start and end apart: 29, of which 9 were waited for; matrix products, arithmetic and copies ran while one was open for 3% of the time, Pallas kernels for 33%

commit v1 on v0

--- a/solution.py
+++ b/solution.py
@@ -245,7 +245,8 @@
             problems.append((q_ref[:, c], k[:, c], g_ref[:, c], v[:, c], lse, row_dot))
     done = gradients(problems)
     for part, (_, c) in enumerate(heads_of(0, 5)):
-        dq_ref[:, c] = sum(dot_nn(ds, k[:, c]) for (_, ds), k in zip(done[4 * part :], k_refs))
+        dq = sum(dot_nn(ds, k[:, c]) for (_, ds), k in zip(done[4 * part :], k_refs))
+        dq_ref[:, c] = dq.astype(HALF)
 
 
 def gathered_stats(s_ref, c):
@@ -333,8 +334,10 @@
     done = gradients(problems)
     for part, (_, c) in enumerate(heads_of(0)):
         mine = done[4 * part : 4 * part + 4]
-        dk_ref[:, c] = sum(dot_nn(ds, qg[0, :, c]) for (_, ds), qg in zip(mine, qg_refs))
-        dv_ref[:, c] = sum(dot_nn(prob, qg[1, :, c]) for (prob, _), qg in zip(mine, qg_refs))
+        dk = sum(dot_nn(ds, qg[0, :, c]) for (_, ds), qg in zip(mine, qg_refs))
+        dk_ref[:, c] = dk.astype(HALF)
+        dv = sum(dot_nn(prob, qg[1, :, c]) for (prob, _), qg in zip(mine, qg_refs))
+        dv_ref[:, c] = dv.astype(HALF)
 
 
 def add_kernel(
@@ -347,9 +350,9 @@
         hit = p == target
         rows = back_ref[h // 3, :, pl.ds(pl.multiple_of(h % 3 * HD, HD), HD)]
         lifted = [dot_nn((hit & (tensor == t)).astype(HALF), rows) for t in range(3)]
-        dq_ref[:, c] = (dq_near_ref[:, c] * SCALING + lifted[0]).astype(HALF)
-        dk_ref[:, c] = (dk_near_ref[:, c] * SCALING + lifted[1]).astype(HALF)
-        dv_ref[:, c] = (dv_near_ref[:, c] + lifted[2]).astype(HALF)
+        dq_ref[:, c] = (dq_near_ref[:, c].astype(FULL) * SCALING + lifted[0]).astype(HALF)
+        dk_ref[:, c] = (dk_near_ref[:, c].astype(FULL) * SCALING + lifted[1]).astype(HALF)
+        dv_ref[:, c] = (dv_near_ref[:, c].astype(FULL) + lifted[2]).astype(HALF)
 
 
 COLUMNS = pl.BlockSpec((ROWS, 2 * HD), lambda s, *_: (0, s))
@@ -460,7 +463,7 @@
     both = [both, core(both), both_x, core(both_x)]
     (dq_near,) = call(
         near_query_kernel, "near_query_gradient", 2, [FIVE] * 2 + [LANES] + [FIVE] * 8,
-        [FIVE], [array(*WIDE, dtype=FULL)],
+        [FIVE], [array(*WIDE)],
         (query, grad_out, stat, *keys0, *values0), time=8,
     )
     sel, dq_near = together(sel, dq_near)
@@ -474,7 +477,7 @@
     s0 = [rows, core(rows), sx, core(sx)]
     dk_near, dv_near = call(
         near_key_kernel, "near_key_gradient", 5, [COLUMNS] * 2 + [PAIR] * 4 + [STAT_ROWS] * 4, [COLUMNS] * 2,
-        [array(*WIDE, dtype=FULL)] * 2, (key, value, *both, *s0),
+        [array(*WIDE)] * 2, (key, value, *both, *s0),
     )
     back = over_z(back)
     back, dk_near = together(back, dk_near)

time: 126 us -> 126 us (level)
  no operation moved by 1% of the time
where the time goes in v1:
time: 126 us; the launch traced here: 125 us
  starting transfers between devices  45.9 us (36%)
  Pallas kernels  45.7 us (36%)
  waiting for transfers between devices  13 us (10%)
  blocking collectives  12.4 us (10%)
  local copies, waits for them, and re-layouts  5.63 us (4%)
  other arithmetic  1.47 us (1%)
    pallas_call x8, Pallas kernels, call(): pl.pallas_call(kernel, grid_spec=pltpu.PrefetchScalarGridSpec(num_scalar_...  45.7 us
    ppermute x26, starting transfers between devices, swapped(): lax.ppermute(x, axis, [(i, i ^ mask) for i in range(lax.axis_size(axis))])  32.6 us
    all_to_all x1, blocking collectives, over_z(): lax.all_to_all(parts, 'seqlo', 0, 0, axis_index_groups=groups, tiled=True)  12.4 us
    ppermute x26, waiting for transfers between devices, swapped(): lax.ppermute(x, axis, [(i, i ^ mask) for i in range(lax.axis_size(axis))])  12.3 us
    all_to_all x2, starting transfers between devices, over_z(): lax.all_to_all(parts, 'seqlo', 0, 0, axis_index_groups=groups, tiled=True)  7.28 us
    all_to_all x1, starting transfers between devices, body(): sel = lax.all_to_all(sel, ('seqhi', 'seqlo'), 0, 0, tiled=True)  5.99 us
    unnamed x48, local copies, waits for them, and re-layouts  3.81 us
  transfers between devices with their start and end apart: 29, of which 9 were waited for; matrix products, arithmetic and copies ran while one was open for 3% of the time, Pallas kernels for 33%

profile of v1, /device:TPU:1, one launch (start us, length us, event | category | flops | bytes accessed | tf_op | source)
XLA Modules:
  0.0 125.0 jit_solution(16663474415376778363)
XLA Ops:
  0.6 2.1 %collective-permute-start = (bf16[256,1280]{1,0:T(8,128)(2,1)}, bf16[256,1280]{1,0:T(8,128)(2,1)}, u32[]{:S(2)}, u32[]{:S(2)}) collective-permute-start(bf16[256,1280]{1,0:T(8,128)(2,1)} %k_ref.3), channel_id=1, source_target_pairs={{0,2},{1,3},{2,0},{3,1},{4,6},{5,7},{6,4},{7,5},{8,10},{9,11},{10,... | collective-permute-start | bytes 1966088 | tf_op jit(solution)/shard_map/ppermute | solution.py:23
  2.8 3.6 %pick_rows.1 = bf16[4,144,384]{2,1,0:T(8,128)(2,1)} custom-call(s32[3,10]{1,0:T(4,128)} %off_ref.5, bf16[256,1280]{1,0:T(8,128)(2,1)} %k_ref.3, bf16[256,1280]{1,0:T(8,128)(2,1)} %v_ref.3, bf16[256,1280]{1,0:T(8,128)(2,1)} %q_ref.4, bf16[256,1280]{1,0:T(8,128)(2,1)} %g_ref.5), custom_call_target="tpu_custom_call" | custom-call | flops 1150000 | bytes 100000 | tf_op jit(solution)/shard_map/pick_rows/pallas_call | solution.py:374
  6.4 12.4 %all_to_all.20.zs_ref = bf16[4,144,384]{2,1,0:T(8,128)(2,1)S(1)} all-to-all(bf16[4,144,384]{2,1,0:T(8,128)(2,1)} %pick_rows.1), channel_id=1, replica_groups={{0,8,16,24},{1,9,17,25},{2,10,18,26},{3,11,19,27},{4,12,20,28},{5,13,21..., dimensions={0} | all-to-all | bytes 884736 | tf_op jit(solution)/shard_map/all_to_all | solution.py:402
  19.2 2.7 %collective-permute-done.1 = bf16[4,16,384]{2,1,0:T(8,128)(2,1)S(1)} collective-permute-done((bf16[4,16,384]{2,1,0:T(8,128)(2,1)S(1)}, bf16[4,16,384]{2,1,0:T(8,128)(2,1)S(1)}, u32[]{:S(2)}, u32[]{:S(2)}) %collective-permute-start.1) | collective-permute-done | bytes 49184 | tf_op jit(solution)/shard_map/ppermute | solution.py:23
  21.9 1.9 %collective-permute-start.4 = (bf16[2,4,16,384]{3,2,1,0:T(8,128)(2,1)S(1)}, bf16[2,4,16,384]{3,2,1,0:T(8,128)(2,1)S(1)}, u32[]{:S(2)}, u32[]{:S(2)}) collective-permute-start(bf16[2,4,16,384]{3,2,1,0:T(8,128)(2,1)S(1)} %pad_maximum_fusion.5), channel_id=1, source_target_pairs={{0,6},{1,7},{2,4},{3,5},{4,2},{5,3},{6,0},{7,1},{8,14},{9,15},{10,... | collective-permute-start | bytes 294920 | tf_op jit(solution)/shard_map/ppermute | solution.py:23
  25.3 1.4 %collective-permute-done.4 = bf16[2,4,16,384]{3,2,1,0:T(8,128)(2,1)S(1)} collective-permute-done((bf16[2,4,16,384]{3,2,1,0:T(8,128)(2,1)S(1)}, bf16[2,4,16,384]{3,2,1,0:T(8,128)(2,1)S(1)}, u32[]{:S(2)}, u32[]{:S(2)}) %collective-permute-start.4) | collective-permute-done | bytes 98336 | tf_op jit(solution)/shard_map/ppermute | solution.py:23
  26.7 1.6 %collective-permute-done.3 = bf16[4,64,384]{2,1,0:T(8,128)(2,1)S(1)} collective-permute-done((bf16[4,64,384]{2,1,0:T(8,128)(2,1)S(1)}, bf16[4,64,384]{2,1,0:T(8,128)(2,1)S(1)}, u32[]{:S(2)}, u32[]{:S(2)}) %collective-permute-start.3) | collective-permute-done | bytes 196640 | tf_op jit(solution)/shard_map/ppermute | solution.py:23
  28.4 2.4 %collective-permute-done.2 = bf16[4,64,384]{2,1,0:T(8,128)(2,1)S(1)} collective-permute-done((bf16[4,64,384]{2,1,0:T(8,128)(2,1)S(1)}, bf16[4,64,384]{2,1,0:T(8,128)(2,1)S(1)}, u32[]{:S(2)}, u32[]{:S(2)}) %collective-permute-start.2) | collective-permute-done | bytes 196640 | tf_op jit(solution)/shard_map/ppermute | solution.py:23
  34.0 1.4 %collective-permute-start.6 = (bf16[4,64,384]{2,1,0:T(8,128)(2,1)S(1)}, bf16[4,64,384]{2,1,0:T(8,128)(2,1)S(1)}, u32[]{:S(2)}, u32[]{:S(2)}) collective-permute-start(bf16[4,64,384]{2,1,0:T(8,128)(2,1)S(1)} %reshape.15), channel_id=1, source_target_pairs={{0,32},{32,0},{64,96},{96,64},{1,33},{33,1},{65,97},{97,65},{2,34}... | collective-permute-start | bytes 589832 | tf_op jit(solution)/shard_map/ppermute | solution.py:23
  35.4 2.6 %collective-permute-start.7 = (bf16[4,64,384]{2,1,0:T(8,128)(2,1)S(1)}, bf16[4,64,384]{2,1,0:T(8,128)(2,1)S(1)}, u32[]{:S(2)}, u32[]{:S(2)}) collective-permute-start(bf16[4,64,384]{2,1,0:T(8,128)(2,1)S(1)} %reshape.15), channel_id=1, source_target_pairs={{0,64},{32,96},{64,0},{96,32},{1,65},{33,97},{65,1},{97,33},{2,66}... | collective-permute-start | bytes 589832 | tf_op jit(solution)/shard_map/ppermute | solution.py:23
  39.3 6.7 %collective-permute-start.12 = (bf16[256,1280]{1,0:T(8,128)(2,1)S(1)}, bf16[256,1280]{1,0:T(8,128)(2,1)S(1)}, u32[]{:S(2)}, u32[]{:S(2)}) collective-permute-start(bf16[256,1280]{1,0:T(8,128)(2,1)S(1)} %copy-done.3), channel_id=1, source_target_pairs={{0,1},{1,0},{2,3},{3,2},{4,5},{5,4},{6,7},{7,6},{8,9},{9,8},{10,11... | collective-permute-start | bytes 1966088 | tf_op jit(solution)/shard_map/ppermute | solution.py:23
  47.1 6.7 %collective-permute-start.11 = (bf16[4,4,64,384]{3,2,1,0:T(8,128)(2,1)S(1)}, bf16[4,4,64,384]{3,2,1,0:T(8,128)(2,1)S(1)}, u32[]{:S(2)}, u32[]{:S(2)}) collective-permute-start(bf16[4,4,64,384]{3,2,1,0:T(8,128)(2,1)S(1)} %pad_maximum_fusion.1.refs_4_.refs_8_), channel_id=1, source_target_pairs={{0,1},{1,0},{2,3},{3,2},{4,5},{5,4},{6,7},{7,6},{8,9},{9,8},{10,11... | collective-permute-start | bytes 2359304 | tf_op jit(solution)/shard_map/ppermute | solution.py:23
  54.4 2.4 %collective-permute-done.9.refs_2_ = bf16[2,4,64,384]{3,2,1,0:T(8,128)(2,1)S(1)} collective-permute-done((bf16[2,4,64,384]{3,2,1,0:T(8,128)(2,1)S(1)}, bf16[2,4,64,384]{3,2,1,0:T(8,128)(2,1)S(1)}, u32[]{:S(2)}, u32[]{:S(2)}) %collective-permute-start.9) | collective-permute-done | bytes 393248 | tf_op jit(solution)/shard_map/ppermute | solution.py:23
  58.1 1.9 %collective-permute-start.17 = (bf16[2,4,64,384]{3,2,1,0:T(8,128)(2,1)S(1)}, bf16[2,4,64,384]{3,2,1,0:T(8,128)(2,1)}, u32[]{:S(2)}, u32[]{:S(2)}) collective-permute-start(bf16[2,4,64,384]{3,2,1,0:T(8,128)(2,1)S(1)} %pad_maximum_fusion.3.refs_4_), channel_id=1, source_target_pairs={{0,6},{1,7},{2,4},{3,5},{4,2},{5,3},{6,0},{7,1},{8,14},{9,15},{10,... | collective-permute-start | bytes 1179656 | tf_op jit(solution)/shard_map/ppermute | solution.py:23
  60.0 3.6 %group_forward.1 = f32[4,40,512]{2,1,0:T(8,128)} custom-call(bf16[4,144,384]{2,1,0:T(8,128)(2,1)} %copy-done.5, bf16[2,4,64,384]{3,2,1,0:T(8,128)(2,1)} %copy-done.6, bf16[2,4,64,384]{3,2,1,0:T(8,128)(2,1)} %copy-done.10, bf16[2,4,64,384]{3,2,1,0:T(8,128)(2,1)} %copy-done.11, bf16[2,4,64,384]{3,2,1,0:T(8,128)(2,1)} %copy-done.12, ...), custom_call_target="tpu_custom_call" | custom-call | flops 1150000 | bytes 100000 | tf_op jit(solution)/shard_map/group_forward/pallas_call | solution.py:374
  63.7 3.6 %all-to-all-start.1 = ((f32[4,40,512]{2,1,0:T(8,128)}), f32[4,40,512]{2,1,0:T(8,128)S(1)}, u32[]{:S(2)}, u32[]{:S(2)}) async-start(f32[4,40,512]{2,1,0:T(8,128)} %group_forward.1), calls=%async_computation.1 | async-start | bytes 655360 | tf_op jit(solution)/shard_map/all_to_all | solution.py:402
  68.0 7.1 %near_forward.1 = (f32[256,1280]{1,0:T(8,128)}, f32[2,8,256]{2,1,0:T(8,128)}) custom-call(bf16[256,1280]{1,0:T(8,128)(2,1)} %q_ref.4, bf16[256,1280]{1,0:T(8,128)(2,1)} %k_ref.3, bf16[256,1280]{1,0:T(8,128)(2,1)} %copy-done.16, bf16[256,1280]{1,0:T(8,128)(2,1)} %collective-permute-done.refs_2_, bf16[256,1280]{1,0:T(8,128)(2,1)} %collective-permute-done.13.refs_3_, ...), custom_call_target="tpu_custom_call" | custom-call | flops 1150000 | bytes 100000 | tf_op jit(solution)/shard_map/near_forward/pallas_call | solution.py:374
  75.8 5.4 %merge_levels.1 = (bf16[256,1280]{1,0:T(8,128)(2,1)}, f32[2,256,128]{2,1,0:T(8,128)}, f32[5,8,256]{2,1,0:T(8,128)}, f32[128,2,128]{2,1,0:T(2,128)}) custom-call(s32[3,10]{1,0:T(4,128)} %off_ref.5, f32[256,1280]{1,0:T(8,128)} %get-tuple-element.63.near_ref, f32[2,8,256]{2,1,0:T(8,128)} %get-tuple-element.67.near_stat_ref, bf16[256,1280]{1,0:T(8,128)(2,1)} %g_ref.5, ...), custom_call_target="tpu_custom_call" | custom-call | flops 1150000 | bytes 100000 | tf_op jit(solution)/shard_map/merge_levels/pallas_call | solution.py:374
  81.8 6.0 %all-to-all-start.2 = ((f32[128,2,128]{2,1,0:T(2,128)}), f32[128,2,128]{2,1,0:T(2,128)S(1)}, u32[]{:S(2)}, u32[]{:S(2)}) async-start(f32[128,2,128]{2,1,0:T(2,128)} %get-tuple-element.70), calls=%async_computation.2 | async-start | bytes 262144 | tf_op jit(solution)/shard_map/all_to_all | solution.py:459
  89.6 7.4 %near_query_gradient.1.dq_near_ref = bf16[256,1280]{1,0:T(8,128)(2,1)} custom-call(bf16[256,1280]{1,0:T(8,128)(2,1)} %q_ref.4, bf16[256,1280]{1,0:T(8,128)(2,1)} %g_ref.5, f32[2,256,128]{2,1,0:T(8,128)} %get-tuple-element.73.stat_ref, bf16[256,1280]{1,0:T(8,128)(2,1)} %k_ref.3, bf16[256,1280]{1,0:T(8,128)(2,1)} %copy-done.16, ...), custom_call_target="tpu_custom_call" | custom-call | flops 9200000000 | bytes 100000 | tf_op jit(solution)/shard_map/near_query_gradient/pallas_call | solution.py:374
  99.3 5.7 %group_backward.1 = bf16[4,112,384]{2,1,0:T(8,128)(2,1)} custom-call(bf16[2,4,64,384]{3,2,1,0:T(8,128)(2,1)} %copy-done.6, bf16[2,4,64,384]{3,2,1,0:T(8,128)(2,1)} %copy-done.10, bf16[2,4,64,384]{3,2,1,0:T(8,128)(2,1)} %copy-done.11, bf16[2,4,64,384]{3,2,1,0:T(8,128)(2,1)} %copy-done.12, bf16[2,4,64,384]{3,2,1,0:T(8,128)(2,1)} %copy-done.9, ...), custom_call_target="tpu_custom_call" | custom-call | flops 1150000 | bytes 100000 | tf_op jit(solution)/shard_map/group_backward/pallas_call | solution.py:374
  105.0 3.7 %all-to-all-start.3 = ((bf16[4,112,384]{2,1,0:T(8,128)(2,1)}), bf16[4,112,384]{2,1,0:T(8,128)(2,1)S(1)}, u32[]{:S(2)}, u32[]{:S(2)}) async-start(bf16[4,112,384]{2,1,0:T(8,128)(2,1)} %group_backward.1), calls=%async_computation.3 | async-start | bytes 688128 | tf_op jit(solution)/shard_map/all_to_all | solution.py:402
  111.4 8.8 %near_key_gradient.1 = (bf16[256,1280]{1,0:T(8,128)(2,1)}, bf16[256,1280]{1,0:T(8,128)(2,1)}) custom-call(bf16[256,1280]{1,0:T(8,128)(2,1)} %k_ref.3, bf16[256,1280]{1,0:T(8,128)(2,1)} %v_ref.3, bf16[2,256,1280]{2,1,0:T(8,128)(2,1)} %pad_maximum_fusion.refs_0_, bf16[2,256,1280]{2,1,0:T(8,128)(2,1)} %copy-done.14, ...), custom_call_target="tpu_custom_call" | custom-call | flops 1150000 | bytes 100000 | tf_op jit(solution)/shard_map/near_key_gradient/pallas_call | solution.py:374
  120.9 4.1 %add_levels.1 = (bf16[256,1280]{1,0:T(8,128)(2,1)}, bf16[256,1280]{1,0:T(8,128)(2,1)}, bf16[256,1280]{1,0:T(8,128)(2,1)}) custom-call(s32[3,10]{1,0:T(4,128)} %off_ref.5, bf16[256,1280]{1,0:T(8,128)(2,1)} %near_query_gradient.1.dq_near_ref, bf16[256,1280]{1,0:T(8,128)(2,1)} %get-tuple-element.82.dk_near_ref, ...), custom_call_target="tpu_custom_call" | custom-call | flops 1150000 | bytes 100000 | tf_op jit(solution)/shard_map/add_levels/pallas_call | solution.py:374
  (102 shorter events, 19.0 us)
Async XLA Ops:
  0.6 18.2 %collective-permute-start = (bf16[256,1280]{1,0:T(8,128)(2,1)}, bf16[256,1280]{1,0:T(8,128)(2,1)}, u32[]{:S(2)}, u32[]{:S(2)}) collective-permute-start(bf16[256,1280]{1,0:T(8,128)(2,1)} %k_ref.3), channel_id=1, source_target_pairs={{0,2},{1,3},{2,0},{3,1},{4,6},{5,7},{6,4},{7,5},{8,10},{9,11},{10,... | collective-permute-start | bytes 1966088 | tf_op jit(solution)/shard_map/ppermute | solution.py:23
  21.9 4.8 %collective-permute-start.4 = (bf16[2,4,16,384]{3,2,1,0:T(8,128)(2,1)S(1)}, bf16[2,4,16,384]{3,2,1,0:T(8,128)(2,1)S(1)}, u32[]{:S(2)}, u32[]{:S(2)}) collective-permute-start(bf16[2,4,16,384]{3,2,1,0:T(8,128)(2,1)S(1)} %pad_maximum_fusion.5), channel_id=1, source_target_pairs={{0,6},{1,7},{2,4},{3,5},{4,2},{5,3},{6,0},{7,1},{8,14},{9,15},{10,... | collective-permute-start | bytes 294920 | tf_op jit(solution)/shard_map/ppermute | solution.py:23
  23.8 4.5 %collective-permute-start.3 = (bf16[4,64,384]{2,1,0:T(8,128)(2,1)S(1)}, bf16[4,64,384]{2,1,0:T(8,128)(2,1)S(1)}, u32[]{:S(2)}, u32[]{:S(2)}) collective-permute-start(bf16[4,64,384]{2,1,0:T(8,128)(2,1)S(1)} %get-tuple-element.50), channel_id=1, source_target_pairs={{0,2},{1,3},{2,0},{3,1},{4,6},{5,7},{6,4},{7,5},{8,10},{9,11},{10,... | collective-permute-start | bytes 589832 | tf_op jit(solution)/shard_map/ppermute | solution.py:23
  24.1 6.7 %collective-permute-start.2 = (bf16[4,64,384]{2,1,0:T(8,128)(2,1)S(1)}, bf16[4,64,384]{2,1,0:T(8,128)(2,1)S(1)}, u32[]{:S(2)}, u32[]{:S(2)}) collective-permute-start(bf16[4,64,384]{2,1,0:T(8,128)(2,1)S(1)} %get-tuple-element.49), channel_id=1, source_target_pairs={{0,2},{1,3},{2,0},{3,1},{4,6},{5,7},{6,4},{7,5},{8,10},{9,11},{10,... | collective-permute-start | bytes 589832 | tf_op jit(solution)/shard_map/ppermute | solution.py:23
  30.9 15.1 %collective-permute-start.15 = (bf16[256,1280]{1,0:T(8,128)(2,1)S(1)}, bf16[256,1280]{1,0:T(8,128)(2,1)}, u32[]{:S(2)}, u32[]{:S(2)}) collective-permute-start(bf16[256,1280]{1,0:T(8,128)(2,1)S(1)} %copy-done.4), channel_id=1, source_target_pairs={{0,2},{1,3},{2,0},{3,1},{4,6},{5,7},{6,4},{7,5},{8,10},{9,11},{10,... | collective-permute-start | bytes 1966088 | tf_op jit(solution)/shard_map/ppermute | solution.py:23
  31.2 14.7 %collective-permute-start.5 = (bf16[2,4,64,384]{3,2,1,0:T(8,128)(2,1)S(1)}, bf16[2,4,64,384]{3,2,1,0:T(8,128)(2,1)S(1)}, u32[]{:S(2)}, u32[]{:S(2)}) collective-permute-start(bf16[2,4,64,384]{3,2,1,0:T(8,128)(2,1)S(1)} %pad_maximum_fusion.2.refs_0_), channel_id=1, source_target_pairs={{0,6},{1,7},{2,4},{3,5},{4,2},{5,3},{6,0},{7,1},{8,14},{9,15},{10,... | collective-permute-start | bytes 1179656 | tf_op jit(solution)/shard_map/ppermute | solution.py:23
  34.0 5.2 %collective-permute-start.6 = (bf16[4,64,384]{2,1,0:T(8,128)(2,1)S(1)}, bf16[4,64,384]{2,1,0:T(8,128)(2,1)S(1)}, u32[]{:S(2)}, u32[]{:S(2)}) collective-permute-start(bf16[4,64,384]{2,1,0:T(8,128)(2,1)S(1)} %reshape.15), channel_id=1, source_target_pairs={{0,32},{32,0},{64,96},{96,64},{1,33},{33,1},{65,97},{97,65},{2,34}... | collective-permute-start | bytes 589832 | tf_op jit(solution)/shard_map/ppermute | solution.py:23
  35.4 10.5 %collective-permute-start.7 = (bf16[4,64,384]{2,1,0:T(8,128)(2,1)S(1)}, bf16[4,64,384]{2,1,0:T(8,128)(2,1)S(1)}, u32[]{:S(2)}, u32[]{:S(2)}) collective-permute-start(bf16[4,64,384]{2,1,0:T(8,128)(2,1)S(1)} %reshape.15), channel_id=1, source_target_pairs={{0,64},{32,96},{64,0},{96,32},{1,65},{33,97},{65,1},{97,33},{2,66}... | collective-permute-start | bytes 589832 | tf_op jit(solution)/shard_map/ppermute | solution.py:23
  38.0 7.9 %collective-permute-start.8 = (bf16[4,64,384]{2,1,0:T(8,128)(2,1)S(1)}, bf16[4,64,384]{2,1,0:T(8,128)(2,1)S(1)}, u32[]{:S(2)}, u32[]{:S(2)}) collective-permute-start(bf16[4,64,384]{2,1,0:T(8,128)(2,1)S(1)} %reshape.15), channel_id=1, source_target_pairs={{0,96},{32,64},{64,32},{96,0},{1,97},{33,65},{65,33},{97,1},{2,98}... | collective-permute-start | bytes 589832 | tf_op jit(solution)/shard_map/ppermute | solution.py:23
  39.3 15.0 %collective-permute-start.12 = (bf16[256,1280]{1,0:T(8,128)(2,1)S(1)}, bf16[256,1280]{1,0:T(8,128)(2,1)S(1)}, u32[]{:S(2)}, u32[]{:S(2)}) collective-permute-start(bf16[256,1280]{1,0:T(8,128)(2,1)S(1)} %copy-done.3), channel_id=1, source_target_pairs={{0,1},{1,0},{2,3},{3,2},{4,5},{5,4},{6,7},{7,6},{8,9},{9,8},{10,11... | collective-permute-start | bytes 1966088 | tf_op jit(solution)/shard_map/ppermute | solution.py:23
  46.0 35.2 %collective-permute-start.18 = (bf16[2,256,1280]{2,1,0:T(8,128)(2,1)}, bf16[2,256,1280]{2,1,0:T(8,128)(2,1)}, u32[]{:S(2)}, u32[]{:S(2)}) collective-permute-start(bf16[2,256,1280]{2,1,0:T(8,128)(2,1)} %pad_maximum_fusion.refs_0_), channel_id=1, source_target_pairs={{0,2},{1,3},{2,0},{3,1},{4,6},{5,7},{6,4},{7,5},{8,10},{9,11},{10,... | collective-permute-start | bytes 3932168 | tf_op jit(solution)/shard_map/ppermute | solution.py:23
  47.1 11.0 %collective-permute-start.11 = (bf16[4,4,64,384]{3,2,1,0:T(8,128)(2,1)S(1)}, bf16[4,4,64,384]{3,2,1,0:T(8,128)(2,1)S(1)}, u32[]{:S(2)}, u32[]{:S(2)}) collective-permute-start(bf16[4,4,64,384]{3,2,1,0:T(8,128)(2,1)S(1)} %pad_maximum_fusion.1.refs_4_.refs_8_), channel_id=1, source_target_pairs={{0,1},{1,0},{2,3},{3,2},{4,5},{5,4},{6,7},{7,6},{8,9},{9,8},{10,11... | collective-permute-start | bytes 2359304 | tf_op jit(solution)/shard_map/ppermute | solution.py:23
  54.3 13.0 %collective-permute-start.14 = (bf16[256,1280]{1,0:T(8,128)(2,1)S(1)}, bf16[256,1280]{1,0:T(8,128)(2,1)}, u32[]{:S(2)}, u32[]{:S(2)}) collective-permute-start(bf16[256,1280]{1,0:T(8,128)(2,1)S(1)} %copy-done.4), channel_id=1, source_target_pairs={{0,1},{1,0},{2,3},{3,2},{4,5},{5,4},{6,7},{7,6},{8,9},{9,8},{10,11... | collective-permute-start | bytes 1966088 | tf_op jit(solution)/shard_map/ppermute | solution.py:23
  56.8 11.2 %collective-permute-start.13 = (bf16[256,1280]{1,0:T(8,128)(2,1)}, bf16[256,1280]{1,0:T(8,128)(2,1)}, u32[]{:S(2)}, u32[]{:S(2)}) collective-permute-start(bf16[256,1280]{1,0:T(8,128)(2,1)} %collective-permute-done.refs_2_), channel_id=1, source_target_pairs={{0,1},{1,0},{2,3},{3,2},{4,5},{5,4},{6,7},{7,6},{8,9},{9,8},{10,11... | collective-permute-start | bytes 1966088 | tf_op jit(solution)/shard_map/ppermute | solution.py:23
  57.7 10.2 %collective-permute-start.16 = (bf16[256,1280]{1,0:T(8,128)(2,1)}, bf16[256,1280]{1,0:T(8,128)(2,1)}, u32[]{:S(2)}, u32[]{:S(2)}) collective-permute-start(bf16[256,1280]{1,0:T(8,128)(2,1)} %collective-permute-done.15.refs_6_), channel_id=1, source_target_pairs={{0,1},{1,0},{2,3},{3,2},{4,5},{5,4},{6,7},{7,6},{8,9},{9,8},{10,11... | collective-permute-start | bytes 1966088 | tf_op jit(solution)/shard_map/ppermute | solution.py:23
  58.1 16.9 %collective-permute-start.17 = (bf16[2,4,64,384]{3,2,1,0:T(8,128)(2,1)S(1)}, bf16[2,4,64,384]{3,2,1,0:T(8,128)(2,1)}, u32[]{:S(2)}, u32[]{:S(2)}) collective-permute-start(bf16[2,4,64,384]{3,2,1,0:T(8,128)(2,1)S(1)} %pad_maximum_fusion.3.refs_4_), channel_id=1, source_target_pairs={{0,6},{1,7},{2,4},{3,5},{4,2},{5,3},{6,0},{7,1},{8,14},{9,15},{10,... | collective-permute-start | bytes 1179656 | tf_op jit(solution)/shard_map/ppermute | solution.py:23
  63.7 11.4 %all-to-all-start.1 = ((f32[4,40,512]{2,1,0:T(8,128)}), f32[4,40,512]{2,1,0:T(8,128)S(1)}, u32[]{:S(2)}, u32[]{:S(2)}) async-start(f32[4,40,512]{2,1,0:T(8,128)} %group_forward.1), calls=%async_computation.1 | async-start | bytes 655360 | tf_op jit(solution)/shard_map/all_to_all | solution.py:402
  67.2 43.0 %collective-permute-start.22 = (bf16[2,256,1280]{2,1,0:T(8,128)(2,1)}, bf16[2,256,1280]{2,1,0:T(8,128)(2,1)S(1)}, u32[]{:S(2)}, u32[]{:S(2)}) collective-permute-start(bf16[2,256,1280]{2,1,0:T(8,128)(2,1)} %pad_maximum_fusion.refs_0_), channel_id=1, source_target_pairs={{0,1},{1,0},{2,3},{3,2},{4,5},{5,4},{6,7},{7,6},{8,9},{9,8},{10,11... | collective-permute-start | bytes 3932168 | tf_op jit(solution)/shard_map/ppermute | solution.py:23
  81.2 29.5 %collective-permute-start.23 = (bf16[2,256,1280]{2,1,0:T(8,128)(2,1)}, bf16[2,256,1280]{2,1,0:T(8,128)(2,1)}, u32[]{:S(2)}, u32[]{:S(2)}) collective-permute-start(bf16[2,256,1280]{2,1,0:T(8,128)(2,1)} %collective-permute-done.18.refs_2_), channel_id=1, source_target_pairs={{0,1},{1,0},{2,3},{3,2},{4,5},{5,4},{6,7},{7,6},{8,9},{9,8},{10,11... | collective-permute-start | bytes 3932168 | tf_op jit(solution)/shard_map/ppermute | solution.py:23
  81.7 16.1 %collective-permute-start.20 = (bf16[2,4,64,384]{3,2,1,0:T(8,128)(2,1)S(1)}, bf16[2,4,64,384]{3,2,1,0:T(8,128)(2,1)S(1)}, u32[]{:S(2)}, u32[]{:S(2)}) collective-permute-start(bf16[2,4,64,384]{3,2,1,0:T(8,128)(2,1)S(1)} %pad_maximum_fusion.3.refs_4_), channel_id=1, source_target_pairs={{0,1},{1,0},{2,3},{3,2},{4,5},{5,4},{6,7},{7,6},{8,9},{9,8},{10,11... | collective-permute-start | bytes 1179656 | tf_op jit(solution)/shard_map/ppermute | solution.py:23
  81.8 16.0 %all-to-all-start.2 = ((f32[128,2,128]{2,1,0:T(2,128)}), f32[128,2,128]{2,1,0:T(2,128)S(1)}, u32[]{:S(2)}, u32[]{:S(2)}) async-start(f32[128,2,128]{2,1,0:T(2,128)} %get-tuple-element.70), calls=%async_computation.2 | async-start | bytes 262144 | tf_op jit(solution)/shard_map/all_to_all | solution.py:459
  87.8 10.0 %collective-permute-start.21 = (bf16[2,4,64,384]{3,2,1,0:T(8,128)(2,1)}, bf16[2,4,64,384]{3,2,1,0:T(8,128)(2,1)S(1)}, u32[]{:S(2)}, u32[]{:S(2)}) collective-permute-start(bf16[2,4,64,384]{3,2,1,0:T(8,128)(2,1)} %collective-permute-done.17.refs_5_), channel_id=1, source_target_pairs={{0,1},{1,0},{2,3},{3,2},{4,5},{5,4},{6,7},{7,6},{8,9},{9,8},{10,11... | collective-permute-start | bytes 1179656 | tf_op jit(solution)/shard_map/ppermute | solution.py:23
  88.9 16.1 %collective-permute-start.19 = (f32[5,8,256]{2,1,0:T(8,128)}, f32[5,8,256]{2,1,0:T(8,128)S(1)}, u32[]{:S(2)}, u32[]{:S(2)}) collective-permute-start(f32[5,8,256]{2,1,0:T(8,128)} %get-tuple-element.75.refs_4_), channel_id=1, source_target_pairs={{0,2},{1,3},{2,0},{3,1},{4,6},{5,7},{6,4},{7,5},{8,10},{9,11},{10,... | collective-permute-start | bytes 122888 | tf_op jit(solution)/shard_map/ppermute | solution.py:23
  105.0 15.2 %all-to-all-start.3 = ((bf16[4,112,384]{2,1,0:T(8,128)(2,1)}), bf16[4,112,384]{2,1,0:T(8,128)(2,1)S(1)}, u32[]{:S(2)}, u32[]{:S(2)}) async-start(bf16[4,112,384]{2,1,0:T(8,128)(2,1)} %group_backward.1), calls=%async_computation.3 | async-start | bytes 688128 | tf_op jit(solution)/shard_map/all_to_all | solution.py:402
  (29 other events, 195.3 us)

commit v2 on v1

--- a/solution.py
+++ b/solution.py
@@ -466,15 +466,15 @@
         [FIVE], [array(*WIDE)],
         (query, grad_out, stat, *keys0, *values0), time=8,
     )
-    sel, dq_near = together(sel, dq_near)
+    sel, sx, dq_near = together(sel, sx, dq_near)
     (back,) = call(
         group_backward_kernel, "group_backward", 1,
         [part_spec] * 8 + [y_spec] * 2 + [whole(128, 2, 128)],
         [whole(4, 112, 384)], [array(4, 112, 384)],
         (*a, *b, *y, sel),
     )
-    sx, back = together(sx, back)
     s0 = [rows, core(rows), sx, core(sx)]
+    s0[0], back = together(rows, back)
     dk_near, dv_near = call(
         near_key_kernel, "near_key_gradient", 5, [COLUMNS] * 2 + [PAIR] * 4 + [STAT_ROWS] * 4, [COLUMNS] * 2,
         [array(*WIDE)] * 2, (key, value, *both, *s0),

time: 126 us -> 126 us (level)
  no operation moved by 1% of the time
where the time goes in v2:
time: 126 us; the launch traced here: 125 us
  Pallas kernels  45.7 us (36%)
  starting transfers between devices  45.4 us (36%)
  waiting for transfers between devices  13.6 us (11%)
  blocking collectives  12.4 us (10%)
  local copies, waits for them, and re-layouts  5.63 us (4%)
  other arithmetic  1.47 us (1%)
    pallas_call x8, Pallas kernels, call(): pl.pallas_call(kernel, grid_spec=pltpu.PrefetchScalarGridSpec(num_scalar_...  45.7 us
    ppermute x26, starting transfers between devices, swapped(): lax.ppermute(x, axis, [(i, i ^ mask) for i in range(lax.axis_size(axis))])  32 us
    all_to_all x1, blocking collectives, over_z(): lax.all_to_all(parts, 'seqlo', 0, 0, axis_index_groups=groups, tiled=True)  12.4 us
    ppermute x26, waiting for transfers between devices, swapped(): lax.ppermute(x, axis, [(i, i ^ mask) for i in range(lax.axis_size(axis))])  12.3 us
    all_to_all x2, starting transfers between devices, over_z(): lax.all_to_all(parts, 'seqlo', 0, 0, axis_index_groups=groups, tiled=True)  7.04 us
    all_to_all x1, starting transfers between devices, body(): sel = lax.all_to_all(sel, ('seqhi', 'seqlo'), 0, 0, tiled=True)  6.31 us
    unnamed x48, local copies, waits for them, and re-layouts  3.81 us
  transfers between devices with their start and end apart: 29, of which 9 were waited for; matrix products, arithmetic and copies ran while one was open for 3% of the time, Pallas kernels for 33%

profile of v2, /device:TPU:1, one launch (start us, length us, event | category | flops | bytes accessed | tf_op | source)
XLA Modules:
  0.0 125.1 jit_solution(8744836273034680323)
XLA Ops:
  0.6 2.1 %collective-permute-start = (bf16[256,1280]{1,0:T(8,128)(2,1)}, bf16[256,1280]{1,0:T(8,128)(2,1)}, u32[]{:S(2)}, u32[]{:S(2)}) collective-permute-start(bf16[256,1280]{1,0:T(8,128)(2,1)} %k_ref.3), channel_id=1, source_target_pairs={{0,2},{1,3},{2,0},{3,1},{4,6},{5,7},{6,4},{7,5},{8,10},{9,11},{10,... | collective-permute-start | bytes 1966088 | tf_op jit(solution)/shard_map/ppermute | solution.py:23
  2.8 3.6 %pick_rows.1 = bf16[4,144,384]{2,1,0:T(8,128)(2,1)} custom-call(s32[3,10]{1,0:T(4,128)} %off_ref.5, bf16[256,1280]{1,0:T(8,128)(2,1)} %k_ref.3, bf16[256,1280]{1,0:T(8,128)(2,1)} %v_ref.3, bf16[256,1280]{1,0:T(8,128)(2,1)} %q_ref.4, bf16[256,1280]{1,0:T(8,128)(2,1)} %g_ref.5), custom_call_target="tpu_custom_call" | custom-call | flops 1150000 | bytes 100000 | tf_op jit(solution)/shard_map/pick_rows/pallas_call | solution.py:374
  6.4 12.4 %all_to_all.20.zs_ref = bf16[4,144,384]{2,1,0:T(8,128)(2,1)S(1)} all-to-all(bf16[4,144,384]{2,1,0:T(8,128)(2,1)} %pick_rows.1), channel_id=1, replica_groups={{0,8,16,24},{1,9,17,25},{2,10,18,26},{3,11,19,27},{4,12,20,28},{5,13,21..., dimensions={0} | all-to-all | bytes 884736 | tf_op jit(solution)/shard_map/all_to_all | solution.py:402
  19.2 2.7 %collective-permute-done.1 = bf16[4,16,384]{2,1,0:T(8,128)(2,1)S(1)} collective-permute-done((bf16[4,16,384]{2,1,0:T(8,128)(2,1)S(1)}, bf16[4,16,384]{2,1,0:T(8,128)(2,1)S(1)}, u32[]{:S(2)}, u32[]{:S(2)}) %collective-permute-start.1) | collective-permute-done | bytes 49184 | tf_op jit(solution)/shard_map/ppermute | solution.py:23
  21.9 1.9 %collective-permute-start.4 = (bf16[2,4,16,384]{3,2,1,0:T(8,128)(2,1)S(1)}, bf16[2,4,16,384]{3,2,1,0:T(8,128)(2,1)S(1)}, u32[]{:S(2)}, u32[]{:S(2)}) collective-permute-start(bf16[2,4,16,384]{3,2,1,0:T(8,128)(2,1)S(1)} %pad_maximum_fusion.5), channel_id=1, source_target_pairs={{0,6},{1,7},{2,4},{3,5},{4,2},{5,3},{6,0},{7,1},{8,14},{9,15},{10,... | collective-permute-start | bytes 294920 | tf_op jit(solution)/shard_map/ppermute | solution.py:23
  25.3 1.4 %collective-permute-done.4 = bf16[2,4,16,384]{3,2,1,0:T(8,128)(2,1)S(1)} collective-permute-done((bf16[2,4,16,384]{3,2,1,0:T(8,128)(2,1)S(1)}, bf16[2,4,16,384]{3,2,1,0:T(8,128)(2,1)S(1)}, u32[]{:S(2)}, u32[]{:S(2)}) %collective-permute-start.4) | collective-permute-done | bytes 98336 | tf_op jit(solution)/shard_map/ppermute | solution.py:23
  26.7 1.6 %collective-permute-done.3 = bf16[4,64,384]{2,1,0:T(8,128)(2,1)S(1)} collective-permute-done((bf16[4,64,384]{2,1,0:T(8,128)(2,1)S(1)}, bf16[4,64,384]{2,1,0:T(8,128)(2,1)S(1)}, u32[]{:S(2)}, u32[]{:S(2)}) %collective-permute-start.3) | collective-permute-done | bytes 196640 | tf_op jit(solution)/shard_map/ppermute | solution.py:23
  28.4 2.4 %collective-permute-done.2 = bf16[4,64,384]{2,1,0:T(8,128)(2,1)S(1)} collective-permute-done((bf16[4,64,384]{2,1,0:T(8,128)(2,1)S(1)}, bf16[4,64,384]{2,1,0:T(8,128)(2,1)S(1)}, u32[]{:S(2)}, u32[]{:S(2)}) %collective-permute-start.2) | collective-permute-done | bytes 196640 | tf_op jit(solution)/shard_map/ppermute | solution.py:23
  34.0 1.4 %collective-permute-start.6 = (bf16[4,64,384]{2,1,0:T(8,128)(2,1)S(1)}, bf16[4,64,384]{2,1,0:T(8,128)(2,1)S(1)}, u32[]{:S(2)}, u32[]{:S(2)}) collective-permute-start(bf16[4,64,384]{2,1,0:T(8,128)(2,1)S(1)} %reshape.15), channel_id=1, source_target_pairs={{0,32},{32,0},{64,96},{96,64},{1,33},{33,1},{65,97},{97,65},{2,34}... | collective-permute-start | bytes 589832 | tf_op jit(solution)/shard_map/ppermute | solution.py:23
  35.4 2.6 %collective-permute-start.7 = (bf16[4,64,384]{2,1,0:T(8,128)(2,1)S(1)}, bf16[4,64,384]{2,1,0:T(8,128)(2,1)S(1)}, u32[]{:S(2)}, u32[]{:S(2)}) collective-permute-start(bf16[4,64,384]{2,1,0:T(8,128)(2,1)S(1)} %reshape.15), channel_id=1, source_target_pairs={{0,64},{32,96},{64,0},{96,32},{1,65},{33,97},{65,1},{97,33},{2,66}... | collective-permute-start | bytes 589832 | tf_op jit(solution)/shard_map/ppermute | solution.py:23
  39.3 6.7 %collective-permute-start.12 = (bf16[256,1280]{1,0:T(8,128)(2,1)S(1)}, bf16[256,1280]{1,0:T(8,128)(2,1)S(1)}, u32[]{:S(2)}, u32[]{:S(2)}) collective-permute-start(bf16[256,1280]{1,0:T(8,128)(2,1)S(1)} %copy-done.3), channel_id=1, source_target_pairs={{0,1},{1,0},{2,3},{3,2},{4,5},{5,4},{6,7},{7,6},{8,9},{9,8},{10,11... | collective-permute-start | bytes 1966088 | tf_op jit(solution)/shard_map/ppermute | solution.py:23
  47.1 6.7 %collective-permute-start.11 = (bf16[4,4,64,384]{3,2,1,0:T(8,128)(2,1)S(1)}, bf16[4,4,64,384]{3,2,1,0:T(8,128)(2,1)S(1)}, u32[]{:S(2)}, u32[]{:S(2)}) collective-permute-start(bf16[4,4,64,384]{3,2,1,0:T(8,128)(2,1)S(1)} %pad_maximum_fusion.1.refs_4_.refs_8_), channel_id=1, source_target_pairs={{0,1},{1,0},{2,3},{3,2},{4,5},{5,4},{6,7},{7,6},{8,9},{9,8},{10,11... | collective-permute-start | bytes 2359304 | tf_op jit(solution)/shard_map/ppermute | solution.py:23
  54.4 2.4 %collective-permute-done.9.refs_2_ = bf16[2,4,64,384]{3,2,1,0:T(8,128)(2,1)S(1)} collective-permute-done((bf16[2,4,64,384]{3,2,1,0:T(8,128)(2,1)S(1)}, bf16[2,4,64,384]{3,2,1,0:T(8,128)(2,1)S(1)}, u32[]{:S(2)}, u32[]{:S(2)}) %collective-permute-start.9) | collective-permute-done | bytes 393248 | tf_op jit(solution)/shard_map/ppermute | solution.py:23
  58.1 1.9 %collective-permute-start.17 = (bf16[2,4,64,384]{3,2,1,0:T(8,128)(2,1)S(1)}, bf16[2,4,64,384]{3,2,1,0:T(8,128)(2,1)}, u32[]{:S(2)}, u32[]{:S(2)}) collective-permute-start(bf16[2,4,64,384]{3,2,1,0:T(8,128)(2,1)S(1)} %pad_maximum_fusion.3.refs_4_), channel_id=1, source_target_pairs={{0,6},{1,7},{2,4},{3,5},{4,2},{5,3},{6,0},{7,1},{8,14},{9,15},{10,... | collective-permute-start | bytes 1179656 | tf_op jit(solution)/shard_map/ppermute | solution.py:23
  60.0 3.6 %group_forward.1 = f32[4,40,512]{2,1,0:T(8,128)} custom-call(bf16[4,144,384]{2,1,0:T(8,128)(2,1)} %copy-done.5, bf16[2,4,64,384]{3,2,1,0:T(8,128)(2,1)} %copy-done.6, bf16[2,4,64,384]{3,2,1,0:T(8,128)(2,1)} %copy-done.10, bf16[2,4,64,384]{3,2,1,0:T(8,128)(2,1)} %copy-done.11, bf16[2,4,64,384]{3,2,1,0:T(8,128)(2,1)} %copy-done.12, ...), custom_call_target="tpu_custom_call" | custom-call | flops 1150000 | bytes 100000 | tf_op jit(solution)/shard_map/group_forward/pallas_call | solution.py:374
  63.7 3.6 %all-to-all-start.1 = ((f32[4,40,512]{2,1,0:T(8,128)}), f32[4,40,512]{2,1,0:T(8,128)S(1)}, u32[]{:S(2)}, u32[]{:S(2)}) async-start(f32[4,40,512]{2,1,0:T(8,128)} %group_forward.1), calls=%async_computation.1 | async-start | bytes 655360 | tf_op jit(solution)/shard_map/all_to_all | solution.py:402
  68.0 7.1 %near_forward.1 = (f32[256,1280]{1,0:T(8,128)}, f32[2,8,256]{2,1,0:T(8,128)}) custom-call(bf16[256,1280]{1,0:T(8,128)(2,1)} %q_ref.4, bf16[256,1280]{1,0:T(8,128)(2,1)} %k_ref.3, bf16[256,1280]{1,0:T(8,128)(2,1)} %copy-done.16, bf16[256,1280]{1,0:T(8,128)(2,1)} %collective-permute-done.refs_2_, bf16[256,1280]{1,0:T(8,128)(2,1)} %collective-permute-done.13.refs_3_, ...), custom_call_target="tpu_custom_call" | custom-call | flops 1150000 | bytes 100000 | tf_op jit(solution)/shard_map/near_forward/pallas_call | solution.py:374
  75.8 5.4 %merge_levels.1 = (bf16[256,1280]{1,0:T(8,128)(2,1)}, f32[2,256,128]{2,1,0:T(8,128)}, f32[5,8,256]{2,1,0:T(8,128)}, f32[128,2,128]{2,1,0:T(2,128)}) custom-call(s32[3,10]{1,0:T(4,128)} %off_ref.5, f32[256,1280]{1,0:T(8,128)} %get-tuple-element.64.near_ref, f32[2,8,256]{2,1,0:T(8,128)} %get-tuple-element.68.near_stat_ref, bf16[256,1280]{1,0:T(8,128)(2,1)} %g_ref.5, ...), custom_call_target="tpu_custom_call" | custom-call | flops 1150000 | bytes 100000 | tf_op jit(solution)/shard_map/merge_levels/pallas_call | solution.py:374
  82.0 6.3 %all-to-all-start.2 = ((f32[128,2,128]{2,1,0:T(2,128)}), f32[128,2,128]{2,1,0:T(2,128)S(1)}, u32[]{:S(2)}, u32[]{:S(2)}) async-start(f32[128,2,128]{2,1,0:T(2,128)} %get-tuple-element.71), calls=%async_computation.2 | async-start | bytes 262144 | tf_op jit(solution)/shard_map/all_to_all | solution.py:459
  89.5 7.4 %near_query_gradient.1.dq_near_ref = bf16[256,1280]{1,0:T(8,128)(2,1)} custom-call(bf16[256,1280]{1,0:T(8,128)(2,1)} %q_ref.4, bf16[256,1280]{1,0:T(8,128)(2,1)} %g_ref.5, f32[2,256,128]{2,1,0:T(8,128)} %get-tuple-element.75.stat_ref, bf16[256,1280]{1,0:T(8,128)(2,1)} %k_ref.3, bf16[256,1280]{1,0:T(8,128)(2,1)} %copy-done.16, ...), custom_call_target="tpu_custom_call" | custom-call | flops 9200000000 | bytes 100000 | tf_op jit(solution)/shard_map/near_query_gradient/pallas_call | solution.py:374
  99.8 5.7 %group_backward.1 = bf16[4,112,384]{2,1,0:T(8,128)(2,1)} custom-call(bf16[2,4,64,384]{3,2,1,0:T(8,128)(2,1)} %copy-done.6, bf16[2,4,64,384]{3,2,1,0:T(8,128)(2,1)} %copy-done.10, bf16[2,4,64,384]{3,2,1,0:T(8,128)(2,1)} %copy-done.11, bf16[2,4,64,384]{3,2,1,0:T(8,128)(2,1)} %copy-done.12, bf16[2,4,64,384]{3,2,1,0:T(8,128)(2,1)} %copy-done.9, ...), custom_call_target="tpu_custom_call" | custom-call | flops 1150000 | bytes 100000 | tf_op jit(solution)/shard_map/group_backward/pallas_call | solution.py:374
  105.5 3.5 %all-to-all-start.3 = ((bf16[4,112,384]{2,1,0:T(8,128)(2,1)}), bf16[4,112,384]{2,1,0:T(8,128)(2,1)S(1)}, u32[]{:S(2)}, u32[]{:S(2)}) async-start(bf16[4,112,384]{2,1,0:T(8,128)(2,1)} %group_backward.1), calls=%async_computation.3 | async-start | bytes 688128 | tf_op jit(solution)/shard_map/all_to_all | solution.py:402
  111.5 8.8 %near_key_gradient.1 = (bf16[256,1280]{1,0:T(8,128)(2,1)}, bf16[256,1280]{1,0:T(8,128)(2,1)}) custom-call(bf16[256,1280]{1,0:T(8,128)(2,1)} %k_ref.3, bf16[256,1280]{1,0:T(8,128)(2,1)} %v_ref.3, bf16[2,256,1280]{2,1,0:T(8,128)(2,1)} %pad_maximum_fusion.refs_0_, bf16[2,256,1280]{2,1,0:T(8,128)(2,1)} %copy-done.14, ...), custom_call_target="tpu_custom_call" | custom-call | flops 1150000 | bytes 100000 | tf_op jit(solution)/shard_map/near_key_gradient/pallas_call | solution.py:374
  121.0 4.1 %add_levels.1 = (bf16[256,1280]{1,0:T(8,128)(2,1)}, bf16[256,1280]{1,0:T(8,128)(2,1)}, bf16[256,1280]{1,0:T(8,128)(2,1)}) custom-call(s32[3,10]{1,0:T(4,128)} %off_ref.5, bf16[256,1280]{1,0:T(8,128)(2,1)} %near_query_gradient.1.dq_near_ref, bf16[256,1280]{1,0:T(8,128)(2,1)} %get-tuple-element.84.dk_near_ref, ...), custom_call_target="tpu_custom_call" | custom-call | flops 1150000 | bytes 100000 | tf_op jit(solution)/shard_map/add_levels/pallas_call | solution.py:374
  (102 shorter events, 19.0 us)
Async XLA Ops:
  0.6 18.2 %collective-permute-start = (bf16[256,1280]{1,0:T(8,128)(2,1)}, bf16[256,1280]{1,0:T(8,128)(2,1)}, u32[]{:S(2)}, u32[]{:S(2)}) collective-permute-start(bf16[256,1280]{1,0:T(8,128)(2,1)} %k_ref.3), channel_id=1, source_target_pairs={{0,2},{1,3},{2,0},{3,1},{4,6},{5,7},{6,4},{7,5},{8,10},{9,11},{10,... | collective-permute-start | bytes 1966088 | tf_op jit(solution)/shard_map/ppermute | solution.py:23
  21.9 4.8 %collective-permute-start.4 = (bf16[2,4,16,384]{3,2,1,0:T(8,128)(2,1)S(1)}, bf16[2,4,16,384]{3,2,1,0:T(8,128)(2,1)S(1)}, u32[]{:S(2)}, u32[]{:S(2)}) collective-permute-start(bf16[2,4,16,384]{3,2,1,0:T(8,128)(2,1)S(1)} %pad_maximum_fusion.5), channel_id=1, source_target_pairs={{0,6},{1,7},{2,4},{3,5},{4,2},{5,3},{6,0},{7,1},{8,14},{9,15},{10,... | collective-permute-start | bytes 294920 | tf_op jit(solution)/shard_map/ppermute | solution.py:23
  23.8 4.5 %collective-permute-start.3 = (bf16[4,64,384]{2,1,0:T(8,128)(2,1)S(1)}, bf16[4,64,384]{2,1,0:T(8,128)(2,1)S(1)}, u32[]{:S(2)}, u32[]{:S(2)}) collective-permute-start(bf16[4,64,384]{2,1,0:T(8,128)(2,1)S(1)} %get-tuple-element.51), channel_id=1, source_target_pairs={{0,2},{1,3},{2,0},{3,1},{4,6},{5,7},{6,4},{7,5},{8,10},{9,11},{10,... | collective-permute-start | bytes 589832 | tf_op jit(solution)/shard_map/ppermute | solution.py:23
  24.1 6.7 %collective-permute-start.2 = (bf16[4,64,384]{2,1,0:T(8,128)(2,1)S(1)}, bf16[4,64,384]{2,1,0:T(8,128)(2,1)S(1)}, u32[]{:S(2)}, u32[]{:S(2)}) collective-permute-start(bf16[4,64,384]{2,1,0:T(8,128)(2,1)S(1)} %get-tuple-element.50), channel_id=1, source_target_pairs={{0,2},{1,3},{2,0},{3,1},{4,6},{5,7},{6,4},{7,5},{8,10},{9,11},{10,... | collective-permute-start | bytes 589832 | tf_op jit(solution)/shard_map/ppermute | solution.py:23
  30.9 15.1 %collective-permute-start.15 = (bf16[256,1280]{1,0:T(8,128)(2,1)S(1)}, bf16[256,1280]{1,0:T(8,128)(2,1)}, u32[]{:S(2)}, u32[]{:S(2)}) collective-permute-start(bf16[256,1280]{1,0:T(8,128)(2,1)S(1)} %copy-done.4), channel_id=1, source_target_pairs={{0,2},{1,3},{2,0},{3,1},{4,6},{5,7},{6,4},{7,5},{8,10},{9,11},{10,... | collective-permute-start | bytes 1966088 | tf_op jit(solution)/shard_map/ppermute | solution.py:23
  31.2 14.7 %collective-permute-start.5 = (bf16[2,4,64,384]{3,2,1,0:T(8,128)(2,1)S(1)}, bf16[2,4,64,384]{3,2,1,0:T(8,128)(2,1)S(1)}, u32[]{:S(2)}, u32[]{:S(2)}) collective-permute-start(bf16[2,4,64,384]{3,2,1,0:T(8,128)(2,1)S(1)} %pad_maximum_fusion.2.refs_0_), channel_id=1, source_target_pairs={{0,6},{1,7},{2,4},{3,5},{4,2},{5,3},{6,0},{7,1},{8,14},{9,15},{10,... | collective-permute-start | bytes 1179656 | tf_op jit(solution)/shard_map/ppermute | solution.py:23
  34.0 5.2 %collective-permute-start.6 = (bf16[4,64,384]{2,1,0:T(8,128)(2,1)S(1)}, bf16[4,64,384]{2,1,0:T(8,128)(2,1)S(1)}, u32[]{:S(2)}, u32[]{:S(2)}) collective-permute-start(bf16[4,64,384]{2,1,0:T(8,128)(2,1)S(1)} %reshape.15), channel_id=1, source_target_pairs={{0,32},{32,0},{64,96},{96,64},{1,33},{33,1},{65,97},{97,65},{2,34}... | collective-permute-start | bytes 589832 | tf_op jit(solution)/shard_map/ppermute | solution.py:23
  35.4 10.5 %collective-permute-start.7 = (bf16[4,64,384]{2,1,0:T(8,128)(2,1)S(1)}, bf16[4,64,384]{2,1,0:T(8,128)(2,1)S(1)}, u32[]{:S(2)}, u32[]{:S(2)}) collective-permute-start(bf16[4,64,384]{2,1,0:T(8,128)(2,1)S(1)} %reshape.15), channel_id=1, source_target_pairs={{0,64},{32,96},{64,0},{96,32},{1,65},{33,97},{65,1},{97,33},{2,66}... | collective-permute-start | bytes 589832 | tf_op jit(solution)/shard_map/ppermute | solution.py:23
  38.0 7.9 %collective-permute-start.8 = (bf16[4,64,384]{2,1,0:T(8,128)(2,1)S(1)}, bf16[4,64,384]{2,1,0:T(8,128)(2,1)S(1)}, u32[]{:S(2)}, u32[]{:S(2)}) collective-permute-start(bf16[4,64,384]{2,1,0:T(8,128)(2,1)S(1)} %reshape.15), channel_id=1, source_target_pairs={{0,96},{32,64},{64,32},{96,0},{1,97},{33,65},{65,33},{97,1},{2,98}... | collective-permute-start | bytes 589832 | tf_op jit(solution)/shard_map/ppermute | solution.py:23
  39.3 15.0 %collective-permute-start.12 = (bf16[256,1280]{1,0:T(8,128)(2,1)S(1)}, bf16[256,1280]{1,0:T(8,128)(2,1)S(1)}, u32[]{:S(2)}, u32[]{:S(2)}) collective-permute-start(bf16[256,1280]{1,0:T(8,128)(2,1)S(1)} %copy-done.3), channel_id=1, source_target_pairs={{0,1},{1,0},{2,3},{3,2},{4,5},{5,4},{6,7},{7,6},{8,9},{9,8},{10,11... | collective-permute-start | bytes 1966088 | tf_op jit(solution)/shard_map/ppermute | solution.py:23
  46.0 35.2 %collective-permute-start.19 = (bf16[2,256,1280]{2,1,0:T(8,128)(2,1)}, bf16[2,256,1280]{2,1,0:T(8,128)(2,1)}, u32[]{:S(2)}, u32[]{:S(2)}) collective-permute-start(bf16[2,256,1280]{2,1,0:T(8,128)(2,1)} %pad_maximum_fusion.refs_0_), channel_id=1, source_target_pairs={{0,2},{1,3},{2,0},{3,1},{4,6},{5,7},{6,4},{7,5},{8,10},{9,11},{10,... | collective-permute-start | bytes 3932168 | tf_op jit(solution)/shard_map/ppermute | solution.py:23
  47.1 11.0 %collective-permute-start.11 = (bf16[4,4,64,384]{3,2,1,0:T(8,128)(2,1)S(1)}, bf16[4,4,64,384]{3,2,1,0:T(8,128)(2,1)S(1)}, u32[]{:S(2)}, u32[]{:S(2)}) collective-permute-start(bf16[4,4,64,384]{3,2,1,0:T(8,128)(2,1)S(1)} %pad_maximum_fusion.1.refs_4_.refs_8_), channel_id=1, source_target_pairs={{0,1},{1,0},{2,3},{3,2},{4,5},{5,4},{6,7},{7,6},{8,9},{9,8},{10,11... | collective-permute-start | bytes 2359304 | tf_op jit(solution)/shard_map/ppermute | solution.py:23
  54.3 13.0 %collective-permute-start.14 = (bf16[256,1280]{1,0:T(8,128)(2,1)S(1)}, bf16[256,1280]{1,0:T(8,128)(2,1)}, u32[]{:S(2)}, u32[]{:S(2)}) collective-permute-start(bf16[256,1280]{1,0:T(8,128)(2,1)S(1)} %copy-done.4), channel_id=1, source_target_pairs={{0,1},{1,0},{2,3},{3,2},{4,5},{5,4},{6,7},{7,6},{8,9},{9,8},{10,11... | collective-permute-start | bytes 1966088 | tf_op jit(solution)/shard_map/ppermute | solution.py:23
  56.8 11.2 %collective-permute-start.13 = (bf16[256,1280]{1,0:T(8,128)(2,1)}, bf16[256,1280]{1,0:T(8,128)(2,1)}, u32[]{:S(2)}, u32[]{:S(2)}) collective-permute-start(bf16[256,1280]{1,0:T(8,128)(2,1)} %collective-permute-done.refs_2_), channel_id=1, source_target_pairs={{0,1},{1,0},{2,3},{3,2},{4,5},{5,4},{6,7},{7,6},{8,9},{9,8},{10,11... | collective-permute-start | bytes 1966088 | tf_op jit(solution)/shard_map/ppermute | solution.py:23
  57.7 10.2 %collective-permute-start.16 = (bf16[256,1280]{1,0:T(8,128)(2,1)}, bf16[256,1280]{1,0:T(8,128)(2,1)}, u32[]{:S(2)}, u32[]{:S(2)}) collective-permute-start(bf16[256,1280]{1,0:T(8,128)(2,1)} %collective-permute-done.15.refs_6_), channel_id=1, source_target_pairs={{0,1},{1,0},{2,3},{3,2},{4,5},{5,4},{6,7},{7,6},{8,9},{9,8},{10,11... | collective-permute-start | bytes 1966088 | tf_op jit(solution)/shard_map/ppermute | solution.py:23
  58.1 16.9 %collective-permute-start.17 = (bf16[2,4,64,384]{3,2,1,0:T(8,128)(2,1)S(1)}, bf16[2,4,64,384]{3,2,1,0:T(8,128)(2,1)}, u32[]{:S(2)}, u32[]{:S(2)}) collective-permute-start(bf16[2,4,64,384]{3,2,1,0:T(8,128)(2,1)S(1)} %pad_maximum_fusion.3.refs_4_), channel_id=1, source_target_pairs={{0,6},{1,7},{2,4},{3,5},{4,2},{5,3},{6,0},{7,1},{8,14},{9,15},{10,... | collective-permute-start | bytes 1179656 | tf_op jit(solution)/shard_map/ppermute | solution.py:23
  63.7 11.4 %all-to-all-start.1 = ((f32[4,40,512]{2,1,0:T(8,128)}), f32[4,40,512]{2,1,0:T(8,128)S(1)}, u32[]{:S(2)}, u32[]{:S(2)}) async-start(f32[4,40,512]{2,1,0:T(8,128)} %group_forward.1), calls=%async_computation.1 | async-start | bytes 655360 | tf_op jit(solution)/shard_map/all_to_all | solution.py:402
  67.2 43.2 %collective-permute-start.22 = (bf16[2,256,1280]{2,1,0:T(8,128)(2,1)}, bf16[2,256,1280]{2,1,0:T(8,128)(2,1)S(1)}, u32[]{:S(2)}, u32[]{:S(2)}) collective-permute-start(bf16[2,256,1280]{2,1,0:T(8,128)(2,1)} %pad_maximum_fusion.refs_0_), channel_id=1, source_target_pairs={{0,1},{1,0},{2,3},{3,2},{4,5},{5,4},{6,7},{7,6},{8,9},{9,8},{10,11... | collective-permute-start | bytes 3932168 | tf_op jit(solution)/shard_map/ppermute | solution.py:23
  81.2 29.6 %collective-permute-start.23 = (bf16[2,256,1280]{2,1,0:T(8,128)(2,1)}, bf16[2,256,1280]{2,1,0:T(8,128)(2,1)}, u32[]{:S(2)}, u32[]{:S(2)}) collective-permute-start(bf16[2,256,1280]{2,1,0:T(8,128)(2,1)} %collective-permute-done.19.refs_2_), channel_id=1, source_target_pairs={{0,1},{1,0},{2,3},{3,2},{4,5},{5,4},{6,7},{7,6},{8,9},{9,8},{10,11... | collective-permute-start | bytes 3932168 | tf_op jit(solution)/shard_map/ppermute | solution.py:23
  81.7 16.6 %collective-permute-start.20 = (bf16[2,4,64,384]{3,2,1,0:T(8,128)(2,1)S(1)}, bf16[2,4,64,384]{3,2,1,0:T(8,128)(2,1)S(1)}, u32[]{:S(2)}, u32[]{:S(2)}) collective-permute-start(bf16[2,4,64,384]{3,2,1,0:T(8,128)(2,1)S(1)} %pad_maximum_fusion.3.refs_4_), channel_id=1, source_target_pairs={{0,1},{1,0},{2,3},{3,2},{4,5},{5,4},{6,7},{7,6},{8,9},{9,8},{10,11... | collective-permute-start | bytes 1179656 | tf_op jit(solution)/shard_map/ppermute | solution.py:23
  81.8 15.2 %collective-permute-start.18 = (f32[5,8,256]{2,1,0:T(8,128)}, f32[5,8,256]{2,1,0:T(8,128)S(1)}, u32[]{:S(2)}, u32[]{:S(2)}) collective-permute-start(f32[5,8,256]{2,1,0:T(8,128)} %get-tuple-element.81.refs_4_), channel_id=1, source_target_pairs={{0,2},{1,3},{2,0},{3,1},{4,6},{5,7},{6,4},{7,5},{8,10},{9,11},{10,... | collective-permute-start | bytes 122888 | tf_op jit(solution)/shard_map/ppermute | solution.py:23
  82.0 16.3 %all-to-all-start.2 = ((f32[128,2,128]{2,1,0:T(2,128)}), f32[128,2,128]{2,1,0:T(2,128)S(1)}, u32[]{:S(2)}, u32[]{:S(2)}) async-start(f32[128,2,128]{2,1,0:T(2,128)} %get-tuple-element.71), calls=%async_computation.2 | async-start | bytes 262144 | tf_op jit(solution)/shard_map/all_to_all | solution.py:459
  88.3 10.0 %collective-permute-start.21 = (bf16[2,4,64,384]{3,2,1,0:T(8,128)(2,1)}, bf16[2,4,64,384]{3,2,1,0:T(8,128)(2,1)S(1)}, u32[]{:S(2)}, u32[]{:S(2)}) collective-permute-start(bf16[2,4,64,384]{3,2,1,0:T(8,128)(2,1)} %collective-permute-done.17.refs_5_), channel_id=1, source_target_pairs={{0,1},{1,0},{2,3},{3,2},{4,5},{5,4},{6,7},{7,6},{8,9},{9,8},{10,11... | collective-permute-start | bytes 1179656 | tf_op jit(solution)/shard_map/ppermute | solution.py:23
  105.5 14.7 %all-to-all-start.3 = ((bf16[4,112,384]{2,1,0:T(8,128)(2,1)}), bf16[4,112,384]{2,1,0:T(8,128)(2,1)S(1)}, u32[]{:S(2)}, u32[]{:S(2)}) async-start(bf16[4,112,384]{2,1,0:T(8,128)(2,1)} %group_backward.1), calls=%async_computation.3 | async-start | bytes 688128 | tf_op jit(solution)/shard_map/all_to_all | solution.py:402
  (29 other events, 203.8 us)
